TPU v7x, 256 devices: a whole 4x4x8 slice. The times are simulated.
256 devices in a mesh: section: 16 (over y_lo, z), tensor: 16 (over y_hi, x, core).
Axes of the slice: x: 4, y: 4 (y_hi: 2, y_lo: 2; y = y_hi * 2 + y_lo), z: 8, core: 2. Of those that a mesh axis runs over, the one named last changes fastest.
Arguments:
- encoder_states: bfloat16 [512, 5120], P('section', 'tensor'), may hold values from -6 to 6
- queries: bfloat16 [16, 128, 4096], P('section', None, 'tensor'), may hold values from -8 to 8
- grad_context: bfloat16 [16, 128, 4096], P('section', None, 'tensor'), may hold values from -6 to 6
- key_weight: bfloat16 [16, 5120, 4096], P('section', None, 'tensor'), may hold values from -0.078125 to 0.078125
- value_weight: bfloat16 [16, 5120, 4096], P('section', None, 'tensor'), may hold values from -0.078125 to 0.078125
Outputs:
- context: bfloat16 [16, 128, 4096], P('section', None, 'tensor')
- grad_queries: bfloat16 [16, 128, 4096], P('section', None, 'tensor')
- grad_key_weight: bfloat16 [16, 5120, 4096], P('section', None, 'tensor')
- grad_value_weight: bfloat16 [16, 5120, 4096], P('section', None, 'tensor')
- grad_encoder: bfloat16 [512, 5120], P('section', 'tensor')
All inputs are finite; a program needn't handle non-finite values.
Results may differ from a plain program's by a relative error of at most 0.03.
Values may be sent and summed in bfloat16 or wider, within the bound.
A program may use at most 128 MiB of HBM per device.

v0:
```python
import jax
import jax.numpy as jnp
from jax import lax
from jax.sharding import PartitionSpec as P

HS = 128
SRC = 512
TGT = 128
SEQS = 1


soft_cap = 20.0


def attend(queries, keys, values, grad_context):
    scale = HS ** (-0.5)
    heads = queries.shape[-1] // HS
    query4 = queries.reshape(SEQS, TGT, heads, HS)
    key4 = keys.reshape(SEQS, SRC, heads, HS)
    value4 = values.reshape(SEQS, SRC, heads, HS)
    grad4 = grad_context.reshape(SEQS, TGT, heads, HS)
    raw = jnp.einsum("sthd,skhd->shtk", query4, key4, preferred_element_type=jnp.float32) * scale
    tangent = jnp.tanh(raw / soft_cap)
    weights = jnp.exp(soft_cap * tangent)
    probs = weights / jnp.sum(weights, axis=-1, keepdims=True)
    probs_low = probs.astype(jnp.bfloat16)
    context = jnp.einsum(
        "shtk,skhd->sthd", probs_low, value4, preferred_element_type=jnp.float32
    ).astype(jnp.bfloat16)
    grad_probs = jnp.einsum("sthd,skhd->shtk", grad4, value4, preferred_element_type=jnp.float32)
    grad_values = jnp.einsum(
        "shtk,sthd->skhd", probs_low, grad4, preferred_element_type=jnp.float32
    ).astype(jnp.bfloat16)
    inner = jnp.sum(probs * grad_probs, axis=-1, keepdims=True)
    grad_raw = (probs * (grad_probs - inner) * (1.0 - tangent * tangent) * scale).astype(
        jnp.bfloat16
    )
    grad_queries = jnp.einsum(
        "shtk,skhd->sthd", grad_raw, key4, preferred_element_type=jnp.float32
    ).astype(jnp.bfloat16)
    grad_keys = jnp.einsum(
        "shtk,sthd->skhd", grad_raw, query4, preferred_element_type=jnp.float32
    ).astype(jnp.bfloat16)
    width = heads * HS
    return (
        context.reshape(QTOK_LOCAL(), width),
        grad_queries.reshape(TGT * SEQS, width),
        grad_keys.reshape(SRC * SEQS, width),
        grad_values.reshape(SRC * SEQS, width),
    )


def QTOK_LOCAL():
    return TGT * SEQS


def per_device(encoder_states, queries, grad_context, key_weight, value_weight):
    key_mat = key_weight[0]
    value_mat = value_weight[0]
    local_rows = lax.all_gather(encoder_states, "tensor", axis=1, tiled=True)
    piece = lax.all_gather(local_rows, "section", axis=0, tiled=True)
    keys_full = jnp.dot(piece, key_mat, preferred_element_type=jnp.float32)
    values_full = jnp.dot(piece, value_mat, preferred_element_type=jnp.float32)
    keys = keys_full.astype(jnp.bfloat16)
    values = values_full.astype(jnp.bfloat16)
    context, grad_q, grad_k, grad_v = attend(queries[0], keys, values, grad_context[0])
    contract_rows = (((0,), (0,)), ((), ()))
    grad_kw = lax.dot_general(
        piece, grad_k, contract_rows, preferred_element_type=jnp.float32
    ).astype(jnp.bfloat16)
    grad_vw = lax.dot_general(
        piece, grad_v, contract_rows, preferred_element_type=jnp.float32
    ).astype(jnp.bfloat16)
    contract_cols = (((1,), (1,)), ((), ()))
    total = lax.dot_general(grad_k, key_mat, contract_cols, preferred_element_type=jnp.float32)
    owned = lax.psum_scatter(
        (
            total
            + lax.dot_general(grad_v, value_mat, contract_cols, preferred_element_type=jnp.float32)
        ).astype(jnp.bfloat16),
        "section",
        scatter_dimension=0,
        tiled=True,
    )
    summed = lax.psum_scatter(owned, "tensor", scatter_dimension=1, tiled=True).astype(jnp.float32)
    return (context[None], grad_q[None], grad_kw[None], grad_vw[None], summed.astype(jnp.bfloat16))


def solution(mesh):
    in_specs = (
        P("section", "tensor"),
        P("section", None, "tensor"),
        P("section", None, "tensor"),
        P("section", None, "tensor"),
        P("section", None, "tensor"),
    )
    out_specs = (
        P("section", None, "tensor"),
        P("section", None, "tensor"),
        P("section", None, "tensor"),
        P("section", None, "tensor"),
        P("section", "tensor"),
    )
    return jax.shard_map(
        per_device, mesh=mesh, in_specs=in_specs, out_specs=out_specs, check_vma=False
    )
```

profile of v0, /device:TPU:1, one launch (start us, length us, event | category | flops | bytes accessed | tf_op | source)
XLA Modules:
  0.0 293.6 jit_solution(6280341238336586599)
XLA Ops:
  7.2 0.0 copy-start
  7.2 0.0 all-gather.3.cloned.1.call-start
  7.2 27.1 %all-gather = bf16[16,320,32]{1,2,0:T(8,128)(2,1)S(1)} all-gather(bf16[1,320,32]{1,2,0:T(8,128)(2,1)} %bitcast.127), channel_id=1, replica_groups=mesh['section'=16,'tensor'=16] {'tensor'}, dimensions={0}, use_global_device_ids=true | all-gather | bytes 348160 | tf_op jit(solution)/shard_map/all_gather | solution.py:60
  34.3 0.1 copy.39
  34.5 1.0 reshape.92
  35.5 0.0 all-gather.3.cloned.1.call-update
  35.5 0.0 reduce-scatter.5.cloned.1.call-start
  35.6 1.0 copy.62
  36.5 1.0 copy.63
  37.5 67.5 %all-gather.3.cloned.1.call-done = bf16[512,5120]{1,0:T(8,128)(2,1)} async-done(((bf16[32,5120]{1,0:T(8,128)(2,1)}), bf16[512,5120]{1,0:T(8,128)(2,1)}) %all-gather.3.cloned.1.call-update) | async-done | bytes 5242896 | tf_op jit(solution)/shard_map/all_gather | solution.py:61
  105.0 0.0 copy-start.5
  105.0 5.0 %fusion.16 = bf16[512,256]{0,1:T(8,128)(2,1)S(1)} fusion(bf16[512,5120]{1,0:T(8,128)(2,1)} %all-gather.3.cloned.1.call-done, bf16[1,5120,256]{2,1,0:T(8,128)(2,1)} %param.9), kind=kOutput, calls=%fused_computation.21 | convolution fusion | flops 1342308352 | bytes 8126464 | tf_op jit(solution)/shard_map/dot_general | solution.py:63
  110.0 0.0 copy-start.3
  110.0 1.1 convolution_bitcast_fusion
  111.1 0.0 copy-done
  111.1 0.0 copy-done.5
  111.1 1.6 fusion.19
  112.7 0.0 copy-done.3
  112.7 0.0 copy-start.4
  112.8 0.4 bitcast_reduce_fusion
  113.1 0.3 copy-done.4
  113.4 0.2 convolution_convert_fusion.2
  113.7 2.4 convolution_convert_fusion.3
  116.1 0.0 copy-start.1
  116.1 2.7 fusion.3
  118.8 0.0 copy-done.1
  118.8 4.0 %add_convert_fusion = bf16[512,5120]{1,0:T(8,128)(2,1)} fusion(f32[512,5120]{1,0:T(8,128)S(1)} %fusion.3, bf16[512,256]{0,1:T(8,128)(2,1)S(1)} %bitcast.112, bf16[1,5120,256]{2,1,0:T(8,128)(2,1)S(1)} %copy-done.1), kind=kOutput, calls=%fused_computation.1 | convolution fusion | flops 1347420160 | bytes 18612224 | tf_op jit(solution)/shard_map/dot_general | solution.py:79
  122.9 0.0 reduce-scatter.5.cloned.1.call-update
  122.9 0.2 reduce-scatter.7.cloned.1.call-start
  123.1 1.2 convolution_convert_fusion.5
  124.3 5.5 %fusion.2 = bf16[1,5120,256]{1,2,0:T(8,128)(2,1)} fusion(bf16[512,256]{0,1:T(8,128)(2,1)S(1)} %bitcast.113, bf16[512,5120]{1,0:T(8,128)(2,1)} %all-gather.3.cloned.1.call-done), kind=kOutput, calls=%fused_computation.5 | convolution fusion | flops 1343488000 | bytes 8126464 | tf_op jit(solution)/shard_map/dot_general | solution.py:71
  129.8 71.4 %reduce-scatter.5.cloned.1.call-done = bf16[32,5120]{1,0:T(8,128)(2,1)} async-done(((bf16[512,5120]{1,0:T(8,128)(2,1)}), bf16[32,5120]{1,0:T(8,128)(2,1)}) %reduce-scatter.5.cloned.1.call-update) | async-done | bytes 327696 | tf_op jit(solution)/shard_map/reduce_scatter | solution.py:76
  201.2 2.3 copy.60
  203.5 0.0 copy-start.2
  203.5 0.0 reduce-scatter.7.cloned.1.call-update
  203.6 1.8 convolution_convert_fusion.4
  205.4 0.7 copy.50
  206.1 0.7 copy.51
  206.9 4.4 %copy.53 = bf16[1,5120,256]{2,1,0:T(8,128)(2,1)} copy(bf16[1,5120,256]{1,2,0:T(8,128)(2,1)} %fusion.2) | data formatting | bytes 5242880
  211.2 0.0 copy-done.2
  211.2 5.5 %fusion.1 = bf16[1,5120,256]{1,2,0:T(8,128)(2,1)} fusion(bf16[512,256]{0,1:T(8,128)(2,1)S(1)} %bitcast.115, bf16[512,5120]{1,0:T(8,128)(2,1)} %all-gather.3.cloned.1.call-done), kind=kOutput, calls=%fused_computation.4 | convolution fusion | flops 1343488000 | bytes 8126464 | tf_op jit(solution)/shard_map/dot_general | solution.py:68
  216.8 4.4 %copy.52 = bf16[1,5120,256]{2,1,0:T(8,128)(2,1)} copy(bf16[1,5120,256]{1,2,0:T(8,128)(2,1)} %fusion.1) | data formatting | bytes 5242880
  221.1 64.3 %reduce-scatter.7.cloned.1.call-done = bf16[320,32]{1,0:T(8,128)(2,1)} async-done(((bf16[5120,32]{1,0:T(8,128)(2,1)}), bf16[320,32]{1,0:T(8,128)(2,1)}) %reduce-scatter.7.cloned.1.call-update) | async-done | bytes 20496
  285.5 1.6 copy.61
Async XLA Ops:
  7.2 103.9 %copy-start = (bf16[1,5120,256]{2,1,0:T(8,128)(2,1)S(1)}, bf16[1,5120,256]{2,1,0:T(8,128)(2,1)}, u32[]{:S(2)}) copy-start(bf16[1,5120,256]{2,1,0:T(8,128)(2,1)} %param.8) | copy-start | bytes 7864324
  7.2 97.8 %all-gather.3.cloned.1.call-start = ((), (), s32[]{:S(2)}) async-start(), calls=%async_computation.2 | async-start | bytes 5570560 | tf_op jit(solution)/shard_map/all_gather | solution.py:61
  35.5 165.7 %reduce-scatter.5.cloned.1.call-start = ((), (), s32[]{:S(2)}) async-start(), calls=%async_computation.3 | async-start | bytes 5570560 | tf_op jit(solution)/shard_map/reduce_scatter | solution.py:76
  105.0 6.1 %copy-start.5 = (bf16[512,5120]{1,0:T(8,128)(2,1)S(1)}, bf16[512,5120]{1,0:T(8,128)(2,1)}, u32[]{:S(2)}) copy-start(bf16[512,5120]{1,0:T(8,128)(2,1)} %all-gather.3.cloned.1.call-done) | copy-start | bytes 15728644
  110.0 2.7 copy-start.3
  112.7 0.7 copy-start.4
  116.1 2.7 copy-start.1
  122.9 162.6 %reduce-scatter.7.cloned.1.call-start = ((), (), s32[]{:S(2)}) async-start(), calls=%async_computation.4 | async-start | bytes 1392640
  203.5 7.7 %copy-start.2 = (bf16[2,512,128]{1,2,0:T(8,128)(2,1)S(1)}, bf16[2,512,128]{1,2,0:T(8,128)(2,1)}, u32[]{:S(2)}) copy-start(bf16[2,512,128]{1,2,0:T(8,128)(2,1)} %convolution_convert_fusion.3) | copy-start | bytes 786436
Sparse Core Ops, SparseCore 0:
  35.6 69.3 all-gather.2
  123.0 78.1 reduce-scatter.4
  205.4 80.0 reduce-scatter.6
where the time goes:
time: 295 us; the launch traced here: 294 us
  waiting for transfers between devices  203 us (69%)
  matrix products  31.5 us (11%)
  blocking collectives  27.1 us (9%)
  local copies, waits for them, and re-layouts  17.5 us (6%)
  between operations  13.9 us (5%)
    reduce_scatter x1, waiting for transfers between devices, per_device(): lax.psum_scatter((total + lax.dot_general(grad_v, value_mat, contract_col...  71.4 us
    all_gather x1, waiting for transfers between devices, per_device(): piece = lax.all_gather(local_rows, 'section', axis=0, tiled=True)  67.5 us
    unnamed x4, waiting for transfers between devices  64.4 us
    all_gather x1, blocking collectives, per_device(): local_rows = lax.all_gather(encoder_states, 'tensor', axis=1, tiled=True)  27.1 us
    unnamed x19, local copies, waits for them, and re-layouts  15.5 us
  transfers between devices with their start and end apart: 3, of which 3 were waited for; matrix products, arithmetic and copies ran while one was open for 9% of the time, Pallas kernels for 0%

commit v1 on v0

v1 whole, which is shorter than its diff:
```python
import functools

import jax
import jax.numpy as jnp
from jax import lax
from jax.experimental import pallas as pl
from jax.experimental.pallas import tpu as pltpu
from jax.sharding import PartitionSpec as P

MESH = pl.DeviceIdType.MESH
BF = jnp.bfloat16
F32 = jnp.float32

D = 5120
HS = 128
SRC = 512
TGT = 128
WIDE = 640
PART = WIDE // 2
CA = 256
CB = WIDE - CA
HALF = SRC // 2
UNIT = 16
SOFT_CAP = 20.0
SCALE = HS ** (-0.5)

EX = 0
A_PL = 1
A_Z = 17
B_Z = 31
B_P = 39
B_Q = 43
D_A = 59
D_B = 75
W_X = 91
G_X = 93
R_Q = 94
R_P = 110
R_Z = 114
S_Z = 122
S_PL = 136
FIN = 152
SLOTS = 153

NT = (((1,), (1,)), ((), ()))
TN = (((0,), (0,)), ((), ()))


def dot(a, b):
    return jnp.dot(a, b, preferred_element_type=F32)


def dot_nt(a, b):
    return lax.dot_general(a, b, NT, preferred_element_type=F32)


def dot_tn(a, b):
    return lax.dot_general(a, b, TN, preferred_element_type=F32)


def kernel(
    x_in, q_in, g_in, kw_in, vw_in,
    context, grad_q, grad_kw, grad_vw, grad_x,
    x, kw, vw, kwp, vwp, own_x, other_x, qv, gv,
    kacc, vacc, grads, grads_p, ts, recv_q, recv_p, recv_z, ring, plane, fin, fin_p,
    out_k, out_v,
    send_sem, recv_sem, local_sem, out_sem,
):
    s = lax.axis_index("section")
    t = lax.axis_index("tensor")
    y_lo, z = lax.div(s, 8), lax.rem(s, 8)
    y_hi, c = lax.div(t, 8), lax.rem(t, 2)
    px = lax.rem(lax.div(t, 2), 4)
    py = y_hi * 2 + y_lo
    block = y_hi * 4 + px

    def at(xx, yy, zz, cc):
        return (lax.rem(yy, 2) * 8 + zz, lax.div(yy, 2) * 8 + xx * 2 + cc)

    def shift(dx, dy):
        return lax.rem(px + dx + 4, 4), lax.rem(py + dy + 4, 4)

    def along(cc, dp, dq):
        return shift(dp * (1 - cc) + dq * cc, dp * cc + dq * (1 - cc))

    partner = at(px, py, z, 1 - c)

    def z_at(k):
        return lax.rem(z + k + 8, 8)

    def z_dev(k):
        return at(px, py, z_at(k), c)

    def rows16(cc, u, zz):
        return pl.ds(pl.multiple_of(cc * HALF + u * 128 + zz * UNIT, UNIT), UNIT)

    def remote(src, dst, slot, device):
        return pltpu.make_async_remote_copy(
            src_ref=src, dst_ref=dst, send_sem=send_sem.at[slot], recv_sem=recv_sem.at[slot],
            device_id=device, device_id_type=MESH,
        )

    sent = []

    def send(src, dst, slot, device):
        copy = remote(src, dst, slot, device)
        copy.start()
        sent.append(copy)

    def arrived(dst, slot):
        remote(dst, dst, slot, partner).wait_recv()

    rows_own = pl.ds(pl.multiple_of(c * UNIT, UNIT), UNIT)
    rows_other = pl.ds(pl.multiple_of((1 - c) * UNIT, UNIT), UNIT)
    loads = [
        pltpu.make_async_copy(x_in.at[rows_own], own_x, local_sem.at[0]),
        pltpu.make_async_copy(kw_in.at[0], kw, local_sem.at[1]),
        pltpu.make_async_copy(vw_in.at[0], vw, local_sem.at[2]),
        pltpu.make_async_copy(q_in.at[0], qv, local_sem.at[3]),
        pltpu.make_async_copy(g_in.at[0], gv, local_sem.at[4]),
    ]
    for load in loads:
        load.start()

    barrier = pltpu.get_barrier_semaphore()
    plane_offsets = [(dx, dy) for dy in range(4) for dx in range(4) if dx or dy]
    peers = [partner]
    peers += [z_dev(k) for k in range(1, 8)]
    peers += [at(*shift(dx, dy), z, c) for dx, dy in plane_offsets]
    for peer in peers:
        pl.semaphore_signal(barrier, inc=1, device_id=peer, device_id_type=MESH)
    pl.semaphore_wait(barrier, len(peers))

    send(x_in.at[rows_other], other_x, EX, partner)
    loads[0].wait()
    arrived(other_x, EX)
    mine, theirs = own_x[...].astype(F32), other_x[...].astype(F32)
    first = jnp.where(c == 0, mine, theirs)
    second = jnp.where(c == 0, theirs, mine)
    x[block, rows16(c, y_lo, z), :] = jnp.concatenate([first, second], axis=1).astype(BF)

    def a_unit(ref, xx, yy):
        return ref.at[lax.div(yy, 2) * 4 + xx, rows16(c, lax.rem(yy, 2), z), pl.ds(0, CA)]

    def a_chunk(ref, cc, u, zz):
        return ref.at[:, rows16(cc, u, zz), pl.ds(0, CA)]

    def b_unit(zz):
        return x.at[block, rows16(c, y_lo, zz), pl.ds(CA, CB)]

    def b_block(ref, cc, base, place):
        xx, yy = place
        rows = pl.ds(pl.multiple_of(base + lax.rem(yy, 2) * 128, 128), 128)
        return ref.at[lax.div(yy, 2) * 4 + xx, rows, pl.ds(CA, CB)]

    for k in range(1, 8):
        send(b_unit(z), b_unit(z), B_Z + k, z_dev(k))
    for dx, dy in plane_offsets:
        unit = a_unit(x, px, py)
        send(unit, unit, A_PL + dy * 4 + dx, at(*shift(dx, dy), z, c))

    def share_a(k, u):
        part = a_chunk(x, c, u, z_at(k))
        send(part, part, D_A + (k % 8) * 2 + u, partner)

    def share_b(j, k):
        part = b_block(x, c, c * HALF, along(c, -j, -k))
        send(part, part, D_B + j * 4 + k, partner)

    def spread_b(j):
        part = b_block(x, c, c * HALF, along(c, -j, 0))
        for k in range(1, 4):
            send(part, part, B_Q + j * 4 + k, at(*along(c, 0, k), z, c))
        share_b(j, 0)

    def pass_on(direction, index):
        sign = 1 - 2 * direction
        u = direction if index == 6 else index % 2
        part = a_chunk(x, c, u, z_at(-sign * (index // 2)))
        send(part, part, A_Z + direction * 7 + index, z_dev(sign))

    def ring_arrived(direction, index):
        sign = 1 - 2 * direction
        u = direction if index == 6 else index % 2
        k = -sign * (index // 2 + 1)
        arrived(a_chunk(x, c, u, z_at(k)), A_Z + direction * 7 + index)
        if index + 2 < 6 or (index + 2 == 6 and direction == 0) or (index == 5 and direction == 1):
            pass_on(direction, min(index + 2, 6))
        share_a(k, u)

    for k in range(1, 8):
        arrived(b_unit(z_at(-k)), B_Z + k)
    own_block = b_block(x, c, c * HALF, along(c, 0, 0))
    for k in range(1, 4):
        send(own_block, own_block, B_P + k, at(*along(c, k, 0), z, c))
    spread_b(0)

    for dx, dy in plane_offsets:
        arrived(a_unit(x, *shift(-dx, -dy)), A_PL + dy * 4 + dx)
    for index in range(2):
        pass_on(0, index)
        pass_on(1, index)
    send(kw_in.at[0], kwp, W_X, partner)
    send(vw_in.at[0], vwp, W_X + 1, partner)
    share_a(0, 0)
    share_a(0, 1)

    for j in range(1, 4):
        arrived(b_block(x, c, c * HALF, along(c, -j, 0)), B_P + j)
        spread_b(j)
        if j < 3:
            for index in (2 * j - 2, 2 * j - 1):
                ring_arrived(0, index)
                ring_arrived(1, index)
    for index in (4, 5, 6):
        ring_arrived(0, index)
        ring_arrived(1, index)
        j = index - 4
        for k in range(1, 4):
            arrived(b_block(x, c, c * HALF, along(c, -j, -k)), B_Q + j * 4 + k)
            share_b(j, k)
    for k in range(1, 4):
        arrived(b_block(x, c, c * HALF, along(c, -3, -k)), B_Q + 12 + k)
        share_b(3, k)

    for k in range(8):
        for u in range(2):
            arrived(a_chunk(x, 1 - c, u, z_at(k)), D_A + k * 2 + u)
    for j in range(4):
        for k in range(4):
            arrived(b_block(x, 1 - c, (1 - c) * HALF, along(1 - c, -j, -k)), D_B + j * 4 + k)

    loads[1].wait()
    loads[2].wait()
    for i in range(4):
        wide = jnp.concatenate([x[2 * i], x[2 * i + 1]], axis=1)
        rows = pl.ds(i * 2 * WIDE, 2 * WIDE)
        k_part, v_part = dot(wide, kw[rows, :]), dot(wide, vw[rows, :])
        if i == 0:
            kacc[...], vacc[...] = k_part, v_part
        else:
            kacc[...] += k_part
            vacc[...] += v_part

    loads[3].wait()
    loads[4].wait()
    for head in range(2):
        cols = pl.ds(head * HS, HS)
        query, grad = qv[:, cols], gv[:, cols]
        key, value = kacc[:, cols].astype(BF), vacc[:, cols].astype(BF)
        tangent = jnp.tanh(dot_nt(query, key) * SCALE / SOFT_CAP)
        weights = jnp.exp(SOFT_CAP * tangent)
        probs = weights / jnp.sum(weights, axis=-1, keepdims=True)
        probs_low = probs.astype(BF)
        context[0, :, cols] = dot(probs_low, value).astype(BF)
        grad_probs = dot_nt(grad, value)
        inner = jnp.sum(probs * grad_probs, axis=-1, keepdims=True)
        grad_raw = (probs * (grad_probs - inner) * (1.0 - tangent * tangent) * SCALE).astype(BF)
        grad_q[0, :, cols] = dot(grad_raw, key).astype(BF)
        grads[:, cols] = dot_tn(grad_raw, query).astype(BF)
        grads[:, pl.ds(2 * HS + head * HS, HS)] = dot_tn(probs_low, grad).astype(BF)

    rows_p = pl.ds(pl.multiple_of((1 - c) * HALF, HALF), HALF)
    rows_c = pl.ds(pl.multiple_of(c * HALF, HALF), HALF)
    send(grads.at[rows_p], grads_p, G_X, partner)

    pieces = [(i, out) for i in range(4) for out in range(2)]
    stores = []

    def weight_grad():
        i, out = pieces.pop(0)
        rows = pl.ds(i * 2 * WIDE, 2 * WIDE)
        held, target = ((out_k, grad_kw), (out_v, grad_vw))[out]
        wide = jnp.concatenate([x[2 * i], x[2 * i + 1]], axis=1)
        held[rows, :] = dot_tn(wide, grads[:, pl.ds(out * 256, 256)]).astype(BF)
        store = pltpu.make_async_copy(held.at[rows], target.at[0, rows], out_sem.at[i * 2 + out])
        store.start()
        stores.append(store)

    weight_grad()
    arrived(grads_p, G_X)
    arrived(kwp, W_X)
    arrived(vwp, W_X + 1)

    def term(row_base, rows, feature, width):
        mine = pl.ds(pl.multiple_of(c * HALF + row_base, 128), rows)
        theirs = pl.ds(pl.multiple_of(row_base, 128), rows)
        span = pl.ds(pl.multiple_of(feature, 128), width)
        return (
            dot_nt(grads[mine, 0:256], kw[span, :])
            + dot_nt(grads[mine, 256:512], vw[span, :])
            + dot_nt(grads_p[theirs, 0:256], kwp[span, :])
            + dot_nt(grads_p[theirs, 256:512], vwp[span, :])
        ).astype(BF)

    for i in range(8):
        ts[i, :, 0:CA] = term(0, HALF, i * WIDE, CA)

    def t_chunk(u, zz):
        return a_chunk(ts, 0, u, zz)

    def scatter(direction, index):
        sign = 1 - 2 * direction
        u = direction if index == 0 else (index - 1) % 2 ^ direction
        part = t_chunk(u, z_at(sign * (4 - (index + 1) // 2)))
        send(part, ring.at[direction * 7 + index], S_Z + direction * 7 + index, z_dev(sign))

    def add(direction, index):
        sign = 1 - 2 * direction
        u = direction if index == 0 else (index - 1) % 2 ^ direction
        held = ring.at[direction * 7 + index]
        arrived(held, S_Z + direction * 7 + index)
        rows = rows16(0, u, z_at(sign * (3 - (index + 1) // 2)))
        ts[:, rows, 0:CA] = (ts[:, rows, 0:CA].astype(F32) + held[...].astype(F32)).astype(BF)
        if index < 5:
            scatter(direction, 1 if index == 0 else index + 2)

    for index in (0, 2):
        scatter(0, index)
        scatter(1, index)

    def compute_b(j, k):
        xx, yy = along(c, j, k)
        low = lax.rem(yy, 2) * 128
        chip = lax.div(yy, 2) * 4 + xx
        rows = pl.ds(pl.multiple_of(low, 128), 128)
        ts[chip, rows, CA:WIDE] = term(low, 128, chip * WIDE + CA, CB)

    def send_b(j, k):
        send(
            b_block(ts, c, 0, along(c, j, k)), recv_q.at[j * 3 + k - 1],
            R_Q + j * 4 + k, at(*along(c, 0, k), z, c),
        )

    for j in (1, 2, 3, 0):
        for k in range(1, 4):
            compute_b(j, k)
            send_b(j, k)
        if j == 2:
            add(0, 0)
            add(1, 0)
    for j in (1, 2, 3, 0):
        compute_b(j, 0)

    def sum_b(j):
        xx, yy = along(c, j, 0)
        rows = pl.ds(pl.multiple_of(lax.rem(yy, 2) * 128, 128), 128)
        chip = lax.div(yy, 2) * 4 + xx
        total = ts[chip, rows, CA:WIDE].astype(F32)
        for k in range(1, 4):
            arrived(recv_q.at[j * 3 + k - 1], R_Q + j * 4 + k)
            total = total + recv_q[j * 3 + k - 1].astype(F32)
        ts[chip, rows, CA:WIDE] = total.astype(BF)

    weight_grad()
    for index in (1, 2):
        add(0, index)
        add(1, index)
    weight_grad()
    for index in (3, 4):
        add(0, index)
        add(1, index)
    weight_grad()
    for j in (1, 2, 3):
        sum_b(j)
        send(
            b_block(ts, c, 0, along(c, j, 0)), recv_p.at[j - 1], R_P + j, at(*along(c, j, 0), z, c)
        )
    sum_b(0)
    for index in (5, 6):
        add(0, index)
        add(1, index)
    for dx, dy in plane_offsets:
        xx, yy = shift(dx, dy)
        send(
            a_unit_t(ts, xx, yy, z), plane.at[dy * 4 + dx], S_PL + dy * 4 + dx, at(xx, yy, z, c)
        )
    weight_grad()

    rows_b = pl.ds(pl.multiple_of(y_lo * 128, 128), 128)
    total = ts[block, rows_b, CA:WIDE].astype(F32)
    for j in range(1, 4):
        arrived(recv_p.at[j - 1], R_P + j)
        total = total + recv_p[j - 1].astype(F32)
    ts[block, rows_b, CA:WIDE] = total.astype(BF)
    for k in range(1, 8):
        part = ts.at[block, rows16(0, y_lo, z_at(k)), pl.ds(CA, CB)]
        send(part, recv_z.at[k - 1], R_Z + k, z_dev(k))
    weight_grad()

    rows_own = rows16(0, y_lo, z)
    total = ts[block, rows_own, 0:CA].astype(F32)
    for dx, dy in plane_offsets:
        arrived(plane.at[dy * 4 + dx], S_PL + dy * 4 + dx)
        total = total + plane[dy * 4 + dx].astype(F32)
    fin[:, 0:CA] = total.astype(BF)
    weight_grad()
    total = ts[block, rows_own, CA:WIDE].astype(F32)
    for k in range(1, 8):
        arrived(recv_z.at[k - 1], R_Z + k)
        total = total + recv_z[k - 1].astype(F32)
    fin[:, CA:WIDE] = total.astype(BF)
    send(fin, fin_p, FIN, partner)
    weight_grad()
    arrived(fin_p, FIN)
    mine, theirs = fin[...].astype(F32), fin_p[...].astype(F32)
    whole = jnp.concatenate(
        [jnp.where(c == 0, mine, theirs), jnp.where(c == 0, theirs, mine)], axis=0
    )
    grad_x[...] = jnp.where(c == 0, whole[:, 0:PART], whole[:, PART:WIDE]).astype(BF)

    for copy in sent:
        copy.wait_send()
    for store in stores:
        store.wait()


def a_unit_t(ref, xx, yy, zz):
    row = pl.multiple_of(lax.rem(yy, 2) * 128 + zz * UNIT, UNIT)
    return ref.at[lax.div(yy, 2) * 4 + xx, pl.ds(row, UNIT), pl.ds(0, CA)]


def per_device(encoder_states, queries, grad_context, key_weight, value_weight):
    anywhere = pl.BlockSpec(memory_space=pl.ANY)
    vmem = pl.BlockSpec(memory_space=pltpu.VMEM)
    shape = jax.ShapeDtypeStruct
    return pl.pallas_call(
        kernel,
        out_shape=(
            shape((1, TGT, 256), BF),
            shape((1, TGT, 256), BF),
            shape((1, D, 256), BF),
            shape((1, D, 256), BF),
            shape((32, PART), BF),
        ),
        in_specs=[anywhere] * 5,
        out_specs=(vmem, vmem, anywhere, anywhere, vmem),
        scratch_shapes=[
            pltpu.VMEM((8, SRC, WIDE), BF),
            pltpu.VMEM((D, 256), BF),
            pltpu.VMEM((D, 256), BF),
            pltpu.VMEM((D, 256), BF),
            pltpu.VMEM((D, 256), BF),
            pltpu.VMEM((UNIT, PART), BF),
            pltpu.VMEM((UNIT, PART), BF),
            pltpu.VMEM((TGT, 256), BF),
            pltpu.VMEM((TGT, 256), BF),
            pltpu.VMEM((SRC, 256), F32),
            pltpu.VMEM((SRC, 256), F32),
            pltpu.VMEM((SRC, 512), BF),
            pltpu.VMEM((HALF, 512), BF),
            pltpu.VMEM((8, HALF, WIDE), BF),
            pltpu.VMEM((12, 128, CB), BF),
            pltpu.VMEM((3, 128, CB), BF),
            pltpu.VMEM((7, UNIT, CB), BF),
            pltpu.VMEM((14, 8, UNIT, CA), BF),
            pltpu.VMEM((16, UNIT, CA), BF),
            pltpu.VMEM((UNIT, WIDE), BF),
            pltpu.VMEM((UNIT, WIDE), BF),
            pltpu.VMEM((D, 256), BF),
            pltpu.VMEM((D, 256), BF),
            pltpu.SemaphoreType.DMA((SLOTS,)),
            pltpu.SemaphoreType.DMA((SLOTS,)),
            pltpu.SemaphoreType.DMA((5,)),
            pltpu.SemaphoreType.DMA((8,)),
        ],
        compiler_params=pltpu.CompilerParams(
            collective_id=0, has_side_effects=True, vmem_limit_bytes=56 << 20
        ),
        cost_estimate=pl.CostEstimate(
            flops=8_500_000_000, bytes_accessed=11_000_000, transcendentals=262_144
        ),
        name="cross_attention_step",
    )(encoder_states, queries, grad_context, key_weight, value_weight)


def solution(mesh):
    in_specs = (
        P("section", "tensor"),
        P("section", None, "tensor"),
        P("section", None, "tensor"),
        P("section", None, "tensor"),
        P("section", None, "tensor"),
    )
    out_specs = (
        P("section", None, "tensor"),
        P("section", None, "tensor"),
        P("section", None, "tensor"),
        P("section", None, "tensor"),
        P("section", "tensor"),
    )
    return jax.shard_map(
        per_device, mesh=mesh, in_specs=in_specs, out_specs=out_specs, check_vma=False
    )
```

time: 295 us -> 84.4 us (0.29)
  waiting for transfers between devices: 203 us -> 0 us
  Pallas kernels: 0 us -> 74.9 us
  matrix products: 31.5 us -> 0 us
  blocking collectives: 27.1 us -> 0 us
  between operations: 13.9 us -> 0.65 us
  local copies, waits for them, and re-layouts: 17.5 us -> 8.6 us
    pallas_call x0 -> x1, Pallas kernels: none -> 74.9 us  [per_device(): pl.pallas_call(kernel, out_shape=(shape((1, TGT, 256), BF), shape((1, TGT...]
    reduce_scatter x1 -> x0, waiting for transfers between devices: 71.4 us -> none  [per_device(): lax.psum_scatter((total + lax.dot_general(grad_v, value_mat, contract_col...]
    all_gather x1 -> x0, waiting for transfers between devices: 67.5 us -> none  [per_device(): piece = lax.all_gather(local_rows, 'section', axis=0, tiled=True)]
    unnamed x4 -> x0, waiting for transfers between devices: 64.4 us -> none
    dot_general x12 -> x0, matrix products: 31.5 us -> none  [the longest x1 5.53 us: per_device(): lax.dot_general(piece, grad_k, contract_rows, preferred_element_type=jnp....]
    all_gather x1 -> x0, blocking collectives: 27.1 us -> none  [per_device(): local_rows = lax.all_gather(encoder_states, 'tensor', axis=1, tiled=True)]
    unnamed x19 -> x9, local copies, waits for them, and re-layouts: 15.5 us -> 8.6 us
  transfers between devices with their start and end apart: 3 -> 0, of which waited for: 3 -> 0; matrix products, arithmetic and copies ran while one was open for 9% -> 0% of each run, Pallas kernels for 0% -> 0%
where the time goes in v1:
time: 84.4 us; the launch traced here: 84.2 us
  Pallas kernels  74.9 us (89%)
  local copies, waits for them, and re-layouts  8.6 us (10%)
    pallas_call x1, Pallas kernels, per_device(): pl.pallas_call(kernel, out_shape=(shape((1, TGT, 256), BF), shape((1, TGT...  74.9 us
    unnamed x9, local copies, waits for them, and re-layouts  8.6 us

profile of v1, /device:TPU:1, one launch (start us, length us, event | category | flops | bytes accessed | tf_op | source)
XLA Modules:
  0.0 84.2 jit_solution(14768306453621803447)
XLA Ops:
  0.6 74.9 %cross_attention_step.1 = (bf16[1,128,256]{2,1,0:T(8,128)(2,1)}, bf16[1,128,256]{2,1,0:T(8,128)(2,1)}, bf16[1,5120,256]{2,1,0:T(8,128)(2,1)}, bf16[1,5120,256]{2,1,0:T(8,128)(2,1)}, bf16[32,320]{1,0:T(8,128)(2,1)}) custom-call(bf16[32,320]{1,0:T(8,128)(2,1)} %x_in.1, bf16[1,128,256]{2,1,0:T(8,128)(2,1)} %q_in.1, bf16[1,128,256]{2,1,0:T(8,128)(2,1)} %g_in.1, ...), custom_call_target="tpu_custom_call" | custom-call | flops 8499999744 | bytes 11000000 | tf_op jit(solution)/shard_map/cross_attention_step/pallas_call | solution.py:427
  75.6 1.5 %copy.15 = bf16[1,128,256]{2,1,0:T(8,128)(2,1)} copy(bf16[1,128,256]{2,1,0:T(8,128)(2,1)} %get-tuple-element.10) | data formatting | bytes 131072
  77.1 1.5 %copy.16 = bf16[1,128,256]{2,1,0:T(8,128)(2,1)} copy(bf16[1,128,256]{2,1,0:T(8,128)(2,1)} %get-tuple-element.11) | data formatting | bytes 131072
  78.5 0.0 copy-start
  78.5 3.5 %copy.17 = bf16[1,5120,256]{2,1,0:T(8,128)(2,1)} copy(bf16[1,5120,256]{2,1,0:T(8,128)(2,1)} %get-tuple-element.12) | data formatting | bytes 5242880
  82.1 0.0 copy-done
  82.1 0.0 copy-start.1
  82.1 1.5 %copy.18 = bf16[1,5120,256]{2,1,0:T(8,128)(2,1)} copy(bf16[1,5120,256]{2,1,0:T(8,128)(2,1)S(1)} %copy-done) | data formatting | bytes 5242880
  83.6 0.0 copy-done.1
  83.6 0.6 copy.19
Async XLA Ops:
  78.5 3.6 %copy-start = (bf16[1,5120,256]{2,1,0:T(8,128)(2,1)S(1)}, bf16[1,5120,256]{2,1,0:T(8,128)(2,1)}, u32[]{:S(2)}) copy-start(bf16[1,5120,256]{2,1,0:T(8,128)(2,1)} %get-tuple-element.13) | copy-start | bytes 7864324
  82.1 1.5 %copy-start.1 = (bf16[32,320]{1,0:T(8,128)(2,1)S(1)}, bf16[32,320]{1,0:T(8,128)(2,1)}, u32[]{:S(2)}) copy-start(bf16[32,320]{1,0:T(8,128)(2,1)} %get-tuple-element.14) | copy-start | bytes 61444

commit v2 on v1

v2 whole, which is shorter than its diff:
```python
import functools

import jax
import jax.numpy as jnp
from jax import lax
from jax.experimental import pallas as pl
from jax.experimental.pallas import tpu as pltpu
from jax.sharding import PartitionSpec as P

MESH = pl.DeviceIdType.MESH
BF = jnp.bfloat16
F32 = jnp.float32

D = 5120
HS = 128
SRC = 512
TGT = 128
WIDE = 640
PART = WIDE // 2
CA = 256
CB = WIDE - CA
HALF = SRC // 2
UNIT = 16
SOFT_CAP = 20.0
SCALE = HS ** (-0.5)

EX = 0
A_PL = 1
A_Z = 5
B_Z = 33
B_P = 34
B_Q = 38
SHARE = 42
W_X = 43
G_X = 44
R_Q = 45
R_P = 49
R_Z = 50
S_Z = 51
S_PL = 83
FIN = 84
RECEIVES = 85

OUT_EX, OUT_UNIT, OUT_ROW, OUT_TILE, OUT_BLOCK, OUT_W, OUT_G, OUT_SUM, OUT_TERM, OUT_FIN = range(10)
SENDS = 10

RING_A = ((3, 0), (3, 1), (2, 2), (2, 3), (2, 0), (2, 1), (1, 2), (1, 3), (1, 0), (1, 1), (0, 2), (0, 3), (0, 0), (0, 1))
RING_B = ((2, 0), (2, 1), (3, 2), (3, 3), (1, 0), (1, 1), (2, 2), (2, 3), (0, 0), (0, 1), (1, 2), (1, 3), (0, 2), (0, 3))

NT = (((1,), (1,)), ((), ()))
TN = (((0,), (0,)), ((), ()))


def dot(a, b):
    return jnp.dot(a, b, preferred_element_type=F32)


def dot_nt(a, b):
    return lax.dot_general(a, b, NT, preferred_element_type=F32)


def dot_tn(a, b):
    return lax.dot_general(a, b, TN, preferred_element_type=F32)


def kernel(
    x_in, q_in, g_in, kw_in, vw_in,
    context, grad_q, grad_kw, grad_vw, grad_x,
    x, kw, vw, pair_w, own_x, other_x, qv, gv,
    keys, values, grads, grads_p, ts, recv_q, recv_p, recv_z, ring, plane, fin, fin_p,
    send_sem, recv_sem, local_sem,
):
    s = lax.axis_index("section")
    t = lax.axis_index("tensor")
    y_lo, z = lax.div(s, 8), lax.rem(s, 8)
    y_hi, c = lax.div(t, 8), lax.rem(t, 2)
    px = lax.rem(lax.div(t, 2), 4)
    py = y_hi * 2 + y_lo
    block = y_hi * 4 + px

    def at(xx, yy, zz, cc):
        return (lax.rem(yy, 2) * 8 + zz, lax.div(yy, 2) * 8 + xx * 2 + cc)

    def along(cc, dp, dq):
        dx = dp * (1 - cc) + dq * cc
        high = abs(dq) // 2 * (1 - cc) + abs(dp) // 2 * cc
        low = abs(dq) % 2 * (1 - cc) + abs(dp) % 2 * cc
        yy = (y_hi + high - 2 * y_hi * high) * 2 + y_lo + low - 2 * y_lo * low
        return lax.rem(px + dx + 4, 4), yy

    partner = at(px, py, z, 1 - c)

    def z_at(k):
        return lax.rem(z + k + 8, 8)

    def z_dev(k):
        return at(px, py, z_at(k), c)

    def rows16(cc, u, zz):
        return pl.ds(pl.multiple_of(cc * HALF + u * 128 + zz * UNIT, UNIT), UNIT)

    def remote(src, dst, out, slot, device):
        return pltpu.make_async_remote_copy(
            src_ref=src, dst_ref=dst, send_sem=send_sem.at[out], recv_sem=recv_sem.at[slot],
            device_id=device, device_id_type=MESH,
        )

    def send(src, dst, out, slot, device):
        remote(src, dst, out, slot, device).start()

    def arrived(dst, slot):
        remote(dst, dst, OUT_EX, slot, partner).wait_recv()

    def left(src, out):
        remote(src, src, out, EX, partner).wait_send()

    rows_own = pl.ds(pl.multiple_of(c * UNIT, UNIT), UNIT)
    rows_other = pl.ds(pl.multiple_of((1 - c) * UNIT, UNIT), UNIT)
    loads = [
        pltpu.make_async_copy(x_in.at[rows_own], own_x, local_sem.at[0]),
        pltpu.make_async_copy(kw_in.at[0], kw, local_sem.at[1]),
        pltpu.make_async_copy(vw_in.at[0], vw, local_sem.at[2]),
        pltpu.make_async_copy(q_in.at[0], qv, local_sem.at[3]),
        pltpu.make_async_copy(g_in.at[0], gv, local_sem.at[4]),
    ]
    for load in loads:
        load.start()

    def row_of(m):
        return (1 - y_hi if m // 2 else y_hi), (1 - y_lo if m % 2 else y_lo)

    def in_plane(dx, m):
        high, low = row_of(m)
        return lax.rem(px + dx + 4, 4), high * 2 + low

    plane_offsets = [(dx, m) for m in (0, 1, 3, 2) for dx in (1, 3, 2, 0) if dx or m]

    barrier = pltpu.get_barrier_semaphore()
    peers = [z_dev(k) for k in (4, 3, 5, 2, 6, 1, 7)]
    peers += [at(*in_plane(dx, m), z, c) for dx, m in reversed(plane_offsets)]
    peers += [partner]
    for peer in peers:
        pl.semaphore_signal(barrier, inc=1, device_id=peer, device_id_type=MESH)
    pl.semaphore_wait(barrier, len(peers))

    send(x_in.at[rows_other], other_x, OUT_EX, EX, partner)
    loads[0].wait()
    arrived(other_x, EX)
    mine, theirs = own_x[...].astype(F32), other_x[...].astype(F32)
    first = jnp.where(c == 0, mine, theirs)
    second = jnp.where(c == 0, theirs, mine)
    x[block, rows16(c, y_lo, z), :] = jnp.concatenate([first, second], axis=1).astype(BF)

    def a_unit(ref, cc, place, zz):
        xx, yy = place
        return ref.at[lax.div(yy, 2) * 4 + xx, rows16(cc, lax.rem(yy, 2), zz), pl.ds(0, CA)]

    def a_row(ref, cc, m, zz):
        high, low = row_of(m)
        return ref.at[pl.ds(high * 4, 4), rows16(cc, low, zz), pl.ds(0, CA)]

    def b_unit(zz):
        return x.at[block, rows16(c, y_lo, zz), pl.ds(CA, CB)]

    def b_block(ref, cc, base, place):
        xx, yy = place
        rows = pl.ds(pl.multiple_of(base + lax.rem(yy, 2) * 128, 128), 128)
        return ref.at[lax.div(yy, 2) * 4 + xx, rows, pl.ds(CA, CB)]

    for dx, m in plane_offsets:
        unit = a_unit(x, c, (px, py), z)
        send(unit, unit, OUT_UNIT, A_PL + m, at(*in_plane(dx, m), z, c))
    for k in (1, 7, 2, 6, 3, 5, 4):
        send(b_unit(z), b_unit(z), OUT_TILE, B_Z, z_dev(k))

    def share_a(k, m):
        part = a_row(x, c, m, z_at(k))
        send(part, part, OUT_ROW, SHARE, partner)

    def share_b(j, k):
        part = b_block(x, c, c * HALF, along(c, -j, -k))
        send(part, part, OUT_BLOCK, SHARE, partner)

    def spread_b(j):
        part = b_block(x, c, c * HALF, along(c, -j, 0))
        for k in (1, 3, 2):
            send(part, part, OUT_BLOCK, B_Q + j, at(*along(c, 0, k), z, c))
        share_b(j, 0)

    def ring_slot(direction, step, m):
        return A_Z + direction * 14 + step * 4 + (m if step < 3 else m % 2)

    def pass_on(direction, step, m):
        sign = 1 - 2 * direction
        part = a_row(x, c, m, z_at(-sign * step))
        send(part, part, OUT_ROW, ring_slot(direction, step, m), z_dev(sign))

    def ring_arrived(step, m):
        for direction in range(2):
            if step == 3 and m // 2 != direction:
                continue
            k = -(1 - 2 * direction) * (step + 1)
            arrived(a_row(x, c, m, z_at(k)), ring_slot(direction, step, m))
            if step < 2 or (step == 2 and m // 2 == direction):
                pass_on(direction, step + 1, m)
            share_a(k, m)

    def ring_start(m):
        high, low = row_of(m)
        units = x.at[pl.ds(high * 4, 4 if m else 3), rows16(c, low, z), pl.ds(0, CA)]
        arrived(units, A_PL + m)
        pass_on(0, 0, m)
        pass_on(1, 0, m)
        share_a(0, m)

    ring_start(0)
    ring_start(1)
    arrived(x.at[block, pl.ds(0, 7 * UNIT), pl.ds(CA, CB)], B_Z)
    own_block = b_block(x, c, c * HALF, along(c, 0, 0))
    for k in (1, 3, 2):
        send(own_block, own_block, OUT_BLOCK, B_P + k, at(*along(c, k, 0), z, c))
    ring_start(3)
    ring_start(2)

    def block_arrived(j):
        arrived(b_block(x, c, c * HALF, along(c, -j, 0)), B_P + j)
        spread_b(j)

    def column_arrived(j):
        arrived(x.at[0:3, pl.ds(0, 128), pl.ds(CA, CB)], B_Q + j)
        for k in (1, 3, 2):
            share_b(j, k)

    ring_arrived(0, 0)
    ring_arrived(0, 1)
    spread_b(0)
    ring_arrived(0, 3)
    ring_arrived(0, 2)
    block_arrived(1)
    block_arrived(3)
    ring_arrived(1, 0)
    ring_arrived(1, 1)
    block_arrived(2)
    send(kw_in.at[0], pair_w.at[0], OUT_W, W_X, partner)
    send(vw_in.at[0], pair_w.at[1], OUT_W, W_X, partner)
    ring_arrived(1, 3)
    ring_arrived(1, 2)
    column_arrived(0)
    ring_arrived(2, 0)
    ring_arrived(2, 1)
    column_arrived(1)
    ring_arrived(2, 3)
    ring_arrived(2, 2)
    column_arrived(3)
    for m in (0, 1, 3, 2):
        ring_arrived(3, m)
    column_arrived(2)

    rows_c = pl.ds(pl.multiple_of(c * HALF, HALF), HALF)
    rows_p = pl.ds(pl.multiple_of((1 - c) * HALF, HALF), HALF)

    def project(rows):
        k_sum, v_sum = 0.0, 0.0
        for i in range(4):
            wide = jnp.concatenate([x[2 * i, rows, :], x[2 * i + 1, rows, :]], axis=1)
            span = pl.ds(i * 2 * WIDE, 2 * WIDE)
            k_sum += dot(wide, kw[span, :])
            v_sum += dot(wide, vw[span, :])
        keys[rows, :] = k_sum.astype(BF)
        values[rows, :] = v_sum.astype(BF)

    loads[1].wait()
    loads[2].wait()
    project(rows_c)
    arrived(x.at[:, rows_p, :], SHARE)
    project(rows_p)

    loads[3].wait()
    loads[4].wait()
    for head in range(2):
        cols = pl.ds(head * HS, HS)
        query, grad = qv[:, cols], gv[:, cols]
        key, value = keys[:, cols], values[:, cols]
        tangent = jnp.tanh(dot_nt(query, key) * SCALE / SOFT_CAP)
        weights = jnp.exp(SOFT_CAP * tangent)
        probs = weights / jnp.sum(weights, axis=-1, keepdims=True)
        probs_low = probs.astype(BF)
        context[0, :, cols] = dot(probs_low, value).astype(BF)
        grad_probs = dot_nt(grad, value)
        inner = jnp.sum(probs * grad_probs, axis=-1, keepdims=True)
        grad_raw = (probs * (grad_probs - inner) * (1.0 - tangent * tangent) * SCALE).astype(BF)
        grad_q[0, :, cols] = dot(grad_raw, key).astype(BF)
        grads[:, cols] = dot_tn(grad_raw, query).astype(BF)
        grads[:, pl.ds(2 * HS + head * HS, HS)] = dot_tn(probs_low, grad).astype(BF)

    send(grads.at[rows_p], grads_p, OUT_G, G_X, partner)

    pieces = [(i, out) for i in range(4) for out in range(2)]

    def weight_grad():
        i, out = pieces.pop(0)
        rows = pl.ds(i * 2 * WIDE, 2 * WIDE)
        wide = jnp.concatenate([x[2 * i], x[2 * i + 1]], axis=1)
        target = (grad_kw, grad_vw)[out]
        target[0, rows, :] = dot_tn(wide, grads[:, pl.ds(out * 256, 256)]).astype(BF)

    weight_grad()
    weight_grad()
    arrived(grads_p, G_X)
    arrived(pair_w, W_X)

    def term(feature, width):
        span = pl.ds(pl.multiple_of(feature, 128), width)
        return (
            dot_nt(grads[rows_c, 0:256], kw[span, :])
            + dot_nt(grads[rows_c, 256:512], vw[span, :])
            + dot_nt(grads_p[:, 0:256], pair_w[0, span, :])
            + dot_nt(grads_p[:, 256:512], pair_w[1, span, :])
        ).astype(BF)

    def compute_a(half):
        high = row_of(half * 2)[0]
        for i in range(4):
            chip = high * 4 + i
            ts[chip, :, 0:CA] = term(chip * WIDE, CA)

    def scatter(direction, togo, m):
        sign = 1 - 2 * direction
        index = direction * 16 + (togo - 1) * 4 + m
        send(a_row(ts, 0, m, z_at(sign * togo)), ring.at[index], OUT_SUM, S_Z + index, z_dev(sign))

    def add(direction, togo, m):
        sign = 1 - 2 * direction
        index = direction * 16 + togo * 4 + m
        held = ring.at[index]
        arrived(held, S_Z + index)
        high, low = row_of(m)
        chips, rows = pl.ds(high * 4, 4), rows16(0, low, z_at(sign * togo))
        ts[chips, rows, 0:CA] = (ts[chips, rows, 0:CA].astype(F32) + held[...].astype(F32)).astype(BF)
        if togo:
            scatter(direction, togo, m)

    def ring_event(*steps):
        for step in steps:
            add(0, *RING_A[step])
            add(1, *RING_B[step])

    def send_b(j):
        for k in (1, 3, 2):
            send(
                b_block(ts, c, 0, along(c, j, k)), recv_q.at[j, k - 1],
                OUT_TERM, R_Q + j, at(*along(c, 0, k), z, c),
            )

    def sum_b(j):
        xx, yy = along(c, j, 0)
        rows = pl.ds(pl.multiple_of(lax.rem(yy, 2) * 128, 128), 128)
        chip = lax.div(yy, 2) * 4 + xx
        total = ts[chip, rows, CA:WIDE].astype(F32)
        arrived(recv_q.at[j], R_Q + j)
        for k in range(3):
            total = total + recv_q[j, k].astype(F32)
        ts[chip, rows, CA:WIDE] = total.astype(BF)
        if j:
            part = b_block(ts, c, 0, along(c, j, 0))
            send(part, recv_p.at[j - 1], OUT_TERM, R_P, at(*along(c, j, 0), z, c))

    for chip in range(8):
        ts[chip, :, CA:WIDE] = term(chip * WIDE + CA, CB)
    for j in (1, 3, 2, 0):
        send_b(j)
    compute_a(0)
    for m in (0, 1):
        scatter(0, 4, m)
        scatter(1, 3, m)
    compute_a(1)
    for m in (2, 3):
        scatter(0, 3, m)
        scatter(1, 4, m)
    weight_grad()
    ring_event(0, 1, 2, 3)
    sum_b(1)
    ring_event(4, 5)
    sum_b(3)
    ring_event(6, 7)
    sum_b(2)
    ring_event(8, 9)
    sum_b(0)

    def send_plane(m):
        for dx in (2, 1, 3, 0):
            if dx or m:
                place = in_plane(dx, m)
                send(
                    a_unit(ts, 0, place, z), plane.at[m * 4 + dx - 1],
                    OUT_UNIT, S_PL, at(*place, z, c),
                )

    ring_event(10, 11, 12)
    send_plane(2)
    send_plane(0)
    ring_event(13)
    send_plane(3)
    send_plane(1)
    rows_b = pl.ds(pl.multiple_of(y_lo * 128, 128), 128)
    total = ts[block, rows_b, CA:WIDE].astype(F32)
    arrived(recv_p, R_P)
    for j in range(3):
        total = total + recv_p[j].astype(F32)
    ts[block, rows_b, CA:WIDE] = total.astype(BF)
    for k in (4, 3, 5, 2, 6, 1, 7):
        part = ts.at[block, rows16(0, y_lo, z_at(k)), pl.ds(CA, CB)]
        send(part, recv_z.at[k - 1], OUT_TILE, R_Z, z_dev(k))
    weight_grad()
    weight_grad()
    weight_grad()

    rows_own = rows16(0, y_lo, z)
    total = ts[block, rows_own, 0:CA].astype(F32)
    arrived(plane, S_PL)
    for index in range(15):
        total = total + plane[index].astype(F32)
    fin[:, 0:CA] = total.astype(BF)
    weight_grad()
    total = ts[block, rows_own, CA:WIDE].astype(F32)
    arrived(recv_z, R_Z)
    for index in range(7):
        total = total + recv_z[index].astype(F32)
    fin[:, CA:WIDE] = total.astype(BF)
    send(fin, fin_p, OUT_FIN, FIN, partner)
    weight_grad()
    arrived(fin_p, FIN)
    mine, theirs = fin[...].astype(F32), fin_p[...].astype(F32)
    whole = jnp.concatenate(
        [jnp.where(c == 0, mine, theirs), jnp.where(c == 0, theirs, mine)], axis=0
    )
    grad_x[...] = jnp.where(c == 0, whole[:, 0:PART], whole[:, PART:WIDE]).astype(BF)

    left(other_x, OUT_EX)
    left(kw.at[0 : 30 * UNIT], OUT_UNIT)
    left(x.at[:, 0 : 30 * UNIT, 0:CA], OUT_ROW)
    left(x.at[0, 0 : 14 * UNIT, 0:CB], OUT_TILE)
    left(x.at[:, 0 : 31 * UNIT, 0:CB], OUT_BLOCK)
    left(pair_w, OUT_W)
    left(grads_p, OUT_G)
    left(x.at[0:7, 0:256, 0:CA], OUT_SUM)
    left(x.at[0:4, 0 : 30 * UNIT, 0:CB], OUT_TERM)
    left(fin, OUT_FIN)


def store(*refs):
    sources, targets, sems = refs[:5], refs[5:10], refs[10]
    copies = [
        pltpu.make_async_copy(src, dst, sems.at[i])
        for i, (src, dst) in enumerate(zip(sources, targets))
    ]
    for copy in copies:
        copy.start()
    for copy in copies:
        copy.wait()


def per_device(encoder_states, queries, grad_context, key_weight, value_weight):
    anywhere = pl.BlockSpec(memory_space=pl.ANY)
    vmem = pl.BlockSpec(memory_space=pltpu.VMEM)
    shapes = ((1, TGT, 256), (1, TGT, 256), (1, D, 256), (1, D, 256), (32, PART))
    inputs = [
        pltpu.with_memory_space_constraint(array, pltpu.HBM)
        for array in (encoder_states, queries, grad_context, key_weight, value_weight)
    ]
    results = pl.pallas_call(
        kernel,
        out_shape=tuple(pltpu.VMEM(shape, BF) for shape in shapes),
        in_specs=[pl.BlockSpec(memory_space=pltpu.HBM)] * 5,
        out_specs=(vmem,) * 5,
        scratch_shapes=[
            pltpu.VMEM((8, SRC, WIDE), BF),
            pltpu.VMEM((D, 256), BF),
            pltpu.VMEM((D, 256), BF),
            pltpu.VMEM((2, D, 256), BF),
            pltpu.VMEM((UNIT, PART), BF),
            pltpu.VMEM((UNIT, PART), BF),
            pltpu.VMEM((TGT, 256), BF),
            pltpu.VMEM((TGT, 256), BF),
            pltpu.VMEM((SRC, 256), BF),
            pltpu.VMEM((SRC, 256), BF),
            pltpu.VMEM((SRC, 512), BF),
            pltpu.VMEM((HALF, 512), BF),
            pltpu.VMEM((8, HALF, WIDE), BF),
            pltpu.VMEM((4, 3, 128, CB), BF),
            pltpu.VMEM((3, 128, CB), BF),
            pltpu.VMEM((7, UNIT, CB), BF),
            pltpu.VMEM((32, 4, UNIT, CA), BF),
            pltpu.VMEM((15, UNIT, CA), BF),
            pltpu.VMEM((UNIT, WIDE), BF),
            pltpu.VMEM((UNIT, WIDE), BF),
            pltpu.SemaphoreType.DMA((SENDS,)),
            pltpu.SemaphoreType.DMA((RECEIVES,)),
            pltpu.SemaphoreType.DMA((5,)),
        ],
        compiler_params=pltpu.CompilerParams(
            collective_id=0, has_side_effects=True, vmem_limit_bytes=40 << 20
        ),
        cost_estimate=pl.CostEstimate(
            flops=8_500_000_000, bytes_accessed=11_000_000, transcendentals=262_144
        ),
        name="cross_attention_step",
    )(*inputs)
    results = [pltpu.with_memory_space_constraint(result, pltpu.VMEM) for result in results]
    return pl.pallas_call(
        store,
        out_shape=tuple(jax.ShapeDtypeStruct(shape, BF) for shape in shapes),
        in_specs=[vmem] * 5,
        out_specs=(anywhere,) * 5,
        scratch_shapes=[pltpu.SemaphoreType.DMA((5,))],
        compiler_params=pltpu.CompilerParams(vmem_limit_bytes=4 << 20),
        name="store_outputs",
    )(*results)


def solution(mesh):
    in_specs = (
        P("section", "tensor"),
        P("section", None, "tensor"),
        P("section", None, "tensor"),
        P("section", None, "tensor"),
        P("section", None, "tensor"),
    )
    out_specs = (
        P("section", None, "tensor"),
        P("section", None, "tensor"),
        P("section", None, "tensor"),
        P("section", None, "tensor"),
        P("section", "tensor"),
    )
    return jax.shard_map(
        per_device, mesh=mesh, in_specs=in_specs, out_specs=out_specs, check_vma=False
    )
```

time: 84.4 us -> 69.5 us (0.82)
  local copies, waits for them, and re-layouts: 8.6 us -> 0 us
  Pallas kernels: 74.9 us -> 68.8 us
    unnamed x9 -> x0, local copies, waits for them, and re-layouts: 8.6 us -> none
    pallas_call x1 -> x2, Pallas kernels: 74.9 us -> 68.8 us  [the longest x1 66.4 us: per_device(): pl.pallas_call(kernel, out_shape=tuple((pltpu.VMEM(shape, BF) for shape i...]
where the time goes in v2:
time: 69.5 us
  Pallas kernels  68.8 us (99%)
    pallas_call x1, Pallas kernels, per_device(): pl.pallas_call(kernel, out_shape=tuple((pltpu.VMEM(shape, BF) for shape i...  66.4 us
    pallas_call x1, Pallas kernels, per_device(): pl.pallas_call(store, out_shape=tuple((jax.ShapeDtypeStruct(shape, BF) fo...  2.45 us

profile of v2, /device:TPU:1, one launch (start us, length us, event | category | flops | bytes accessed | tf_op | source)
XLA Modules:
  0.0 69.5 jit_solution(12885425458938275232)
XLA Ops:
  0.6 66.4 %cross_attention_step.1 = (bf16[1,128,256]{2,1,0:T(8,128)(2,1)S(1)}, bf16[1,128,256]{2,1,0:T(8,128)(2,1)S(1)}, bf16[1,5120,256]{2,1,0:T(8,128)(2,1)S(1)}, bf16[1...) custom-call(bf16[32,320]{1,0:T(8,128)(2,1)} %x_in.1, bf16[1,128,256]{2,1,0:T(8,128)(2,1)} %q_in.1, ...), custom_call_target="tpu_custom_call" | custom-call | flops 8499999744 | bytes 11000000 | tf_op jit(solution)/shard_map/cross_attention_step/pallas_call | solution.py:471
  67.0 2.4 %store_outputs.1 = (bf16[1,128,256]{2,1,0:T(8,128)(2,1)}, bf16[1,128,256]{2,1,0:T(8,128)(2,1)}, bf16[1,5120,256]{2,1,0:T(8,128)(2,1)}, bf16[1,5120,256]{2,1,0:T(8,128)(2,1)}, bf16[32,320]{1,0:T(8,128)(2,1)}) custom-call(bf16[1,128,256]{2,1,0:T(8,128)(2,1)S(1)} %get-tuple-element.10.refs_0_, bf16[1,128,256]{2,1,0:T(8,128)(2,1)S(1)} %get-tuple-element.11.refs_1_, ...), custom_call_target="tpu_custom_call" | custom-call | tf_op jit(solution)/shard_map/store_outputs/pallas_call | solution.py:510

commit v3 on v2

--- a/solution.py
+++ b/solution.py
@@ -27,25 +27,27 @@
 EX = 0
 A_PL = 1
 A_Z = 5
-B_Z = 33
-B_P = 34
-B_Q = 38
-SHARE = 42
-W_X = 43
-G_X = 44
-R_Q = 45
-R_P = 49
-R_Z = 50
-S_Z = 51
-S_PL = 83
-FIN = 84
-RECEIVES = 85
+B_Z = 19
+B_P = 20
+B_Q = 24
+SHARE = 28
+W_X = 29
+G_X = 30
+R_Q = 31
+R_P = 35
+R_Z = 36
+S_Z = 37
+S_PL = 51
+FIN = 52
+RECEIVES = 53
 
 OUT_EX, OUT_UNIT, OUT_ROW, OUT_TILE, OUT_BLOCK, OUT_W, OUT_G, OUT_SUM, OUT_TERM, OUT_FIN = range(10)
 SENDS = 10
 
+GATHER_A = ((0, 0), (0, 1), (0, 3), (0, 2), (1, 0), (1, 1), (1, 3), (1, 2), (2, 0), (2, 1), (2, 3), (2, 2), (3, 0), (3, 1))
+GATHER_B = ((0, 0), (0, 3), (0, 2), (0, 1), (1, 3), (1, 2), (1, 0), (1, 1), (2, 3), (2, 2), (2, 0), (2, 1), (3, 3), (3, 2))
 RING_A = ((3, 0), (3, 1), (2, 2), (2, 3), (2, 0), (2, 1), (1, 2), (1, 3), (1, 0), (1, 1), (0, 2), (0, 3), (0, 0), (0, 1))
-RING_B = ((2, 0), (2, 1), (3, 2), (3, 3), (1, 0), (1, 1), (2, 2), (2, 3), (0, 0), (0, 1), (1, 2), (1, 3), (0, 2), (0, 3))
+RING_B = ((2, 0), (3, 2), (3, 3), (2, 1), (2, 2), (2, 3), (1, 0), (1, 2), (1, 3), (1, 1), (0, 0), (0, 2), (0, 3), (0, 1))
 
 NT = (((1,), (1,)), ((), ()))
 TN = (((0,), (0,)), ((), ()))
@@ -66,7 +68,7 @@
 def kernel(
     x_in, q_in, g_in, kw_in, vw_in,
     context, grad_q, grad_kw, grad_vw, grad_x,
-    x, kw, vw, pair_w, own_x, other_x, qv, gv,
+    x, w, own_x, other_x, probs_held, raw_held, own_terms, qv, gv,
     keys, values, grads, grads_p, ts, recv_q, recv_p, recv_z, ring, plane, fin, fin_p,
     send_sem, recv_sem, local_sem,
 ):
@@ -82,9 +84,9 @@
         return (lax.rem(yy, 2) * 8 + zz, lax.div(yy, 2) * 8 + xx * 2 + cc)
 
     def along(cc, dp, dq):
-        dx = dp * (1 - cc) + dq * cc
-        high = abs(dq) // 2 * (1 - cc) + abs(dp) // 2 * cc
-        low = abs(dq) % 2 * (1 - cc) + abs(dp) % 2 * cc
+        dx = dp * cc + dq * (1 - cc)
+        high = abs(dq) // 2 * cc + abs(dp) // 2 * (1 - cc)
+        low = abs(dq) % 2 * cc + abs(dp) % 2 * (1 - cc)
         yy = (y_hi + high - 2 * y_hi * high) * 2 + y_lo + low - 2 * y_lo * low
         return lax.rem(px + dx + 4, 4), yy
 
@@ -117,9 +119,9 @@
     rows_own = pl.ds(pl.multiple_of(c * UNIT, UNIT), UNIT)
     rows_other = pl.ds(pl.multiple_of((1 - c) * UNIT, UNIT), UNIT)
     loads = [
-        pltpu.make_async_copy(x_in.at[rows_own], own_x, local_sem.at[0]),
-        pltpu.make_async_copy(kw_in.at[0], kw, local_sem.at[1]),
-        pltpu.make_async_copy(vw_in.at[0], vw, local_sem.at[2]),
+        pltpu.make_async_copy(x_in, own_x, local_sem.at[0]),
+        pltpu.make_async_copy(kw_in.at[0], w.at[:, 0:256], local_sem.at[1]),
+        pltpu.make_async_copy(vw_in.at[0], w.at[:, 256:512], local_sem.at[2]),
         pltpu.make_async_copy(q_in.at[0], qv, local_sem.at[3]),
         pltpu.make_async_copy(g_in.at[0], gv, local_sem.at[4]),
     ]
@@ -136,17 +138,16 @@
     plane_offsets = [(dx, m) for m in (0, 1, 3, 2) for dx in (1, 3, 2, 0) if dx or m]
 
     barrier = pltpu.get_barrier_semaphore()
-    peers = [z_dev(k) for k in (4, 3, 5, 2, 6, 1, 7)]
-    peers += [at(*in_plane(dx, m), z, c) for dx, m in reversed(plane_offsets)]
-    peers += [partner]
+    peers = [partner] + [z_dev(k) for k in (1, 7, 2, 6, 3, 5, 4)]
+    peers += [at(*in_plane(dx, m), z, c) for dx, m in plane_offsets]
     for peer in peers:
         pl.semaphore_signal(barrier, inc=1, device_id=peer, device_id_type=MESH)
+    loads[0].wait()
     pl.semaphore_wait(barrier, len(peers))
 
-    send(x_in.at[rows_other], other_x, OUT_EX, EX, partner)
-    loads[0].wait()
+    send(own_x.at[rows_other], other_x, OUT_EX, EX, partner)
     arrived(other_x, EX)
-    mine, theirs = own_x[...].astype(F32), other_x[...].astype(F32)
+    mine, theirs = own_x[rows_own, :].astype(F32), other_x[...].astype(F32)
     first = jnp.where(c == 0, mine, theirs)
     second = jnp.where(c == 0, theirs, mine)
     x[block, rows16(c, y_lo, z), :] = jnp.concatenate([first, second], axis=1).astype(BF)
@@ -173,6 +174,11 @@
     for k in (1, 7, 2, 6, 3, 5, 4):
         send(b_unit(z), b_unit(z), OUT_TILE, B_Z, z_dev(k))
 
+    loads[1].wait()
+    loads[2].wait()
+    for i in range(2):
+        send(w.at[:, i * 256 : (i + 1) * 256], w.at[:, (i + 2) * 256 : (i + 3) * 256], OUT_W, W_X, partner)
+
     def share_a(k, m):
         part = a_row(x, c, m, z_at(k))
         send(part, part, OUT_ROW, SHARE, partner)
@@ -187,23 +193,20 @@
             send(part, part, OUT_BLOCK, B_Q + j, at(*along(c, 0, k), z, c))
         share_b(j, 0)
 
-    def ring_slot(direction, step, m):
-        return A_Z + direction * 14 + step * 4 + (m if step < 3 else m % 2)
-
     def pass_on(direction, step, m):
         sign = 1 - 2 * direction
         part = a_row(x, c, m, z_at(-sign * step))
-        send(part, part, OUT_ROW, ring_slot(direction, step, m), z_dev(sign))
-
-    def ring_arrived(step, m):
-        for direction in range(2):
-            if step == 3 and m // 2 != direction:
-                continue
-            k = -(1 - 2 * direction) * (step + 1)
-            arrived(a_row(x, c, m, z_at(k)), ring_slot(direction, step, m))
-            if step < 2 or (step == 2 and m // 2 == direction):
-                pass_on(direction, step + 1, m)
-            share_a(k, m)
+        event = (GATHER_A, GATHER_B)[direction].index((step, m))
+        send(part, part, OUT_ROW, A_Z + event, z_dev(sign))
+
+    def ring_arrived(*events):
+        for event in events:
+            arrived(x.at[:, rows16(c, y_lo, z), pl.ds(0, CA)], A_Z + event)
+            for direction, order in enumerate((GATHER_A, GATHER_B)):
+                step, m = order[event]
+                if step < 2 or (step == 2 and m // 2 == direction):
+                    pass_on(direction, step + 1, m)
+                share_a(-(1 - 2 * direction) * (step + 1), m)
 
     def ring_start(m):
         high, low = row_of(m)
@@ -231,126 +234,115 @@
         for k in (1, 3, 2):
             share_b(j, k)
 
-    ring_arrived(0, 0)
-    ring_arrived(0, 1)
+    ring_arrived(0)
     spread_b(0)
-    ring_arrived(0, 3)
-    ring_arrived(0, 2)
+    ring_arrived(1)
     block_arrived(1)
     block_arrived(3)
-    ring_arrived(1, 0)
-    ring_arrived(1, 1)
+    ring_arrived(2, 3)
     block_arrived(2)
-    send(kw_in.at[0], pair_w.at[0], OUT_W, W_X, partner)
-    send(vw_in.at[0], pair_w.at[1], OUT_W, W_X, partner)
-    ring_arrived(1, 3)
-    ring_arrived(1, 2)
+    ring_arrived(4, 5)
+    ring_arrived(6, 7)
     column_arrived(0)
-    ring_arrived(2, 0)
-    ring_arrived(2, 1)
+    ring_arrived(8, 9)
     column_arrived(1)
-    ring_arrived(2, 3)
-    ring_arrived(2, 2)
+    ring_arrived(10, 11)
     column_arrived(3)
-    for m in (0, 1, 3, 2):
-        ring_arrived(3, m)
+    ring_arrived(12, 13)
     column_arrived(2)
 
     rows_c = pl.ds(pl.multiple_of(c * HALF, HALF), HALF)
     rows_p = pl.ds(pl.multiple_of((1 - c) * HALF, HALF), HALF)
 
     def project(rows):
-        k_sum, v_sum = 0.0, 0.0
+        total = 0.0
         for i in range(4):
             wide = jnp.concatenate([x[2 * i, rows, :], x[2 * i + 1, rows, :]], axis=1)
-            span = pl.ds(i * 2 * WIDE, 2 * WIDE)
-            k_sum += dot(wide, kw[span, :])
-            v_sum += dot(wide, vw[span, :])
-        keys[rows, :] = k_sum.astype(BF)
-        values[rows, :] = v_sum.astype(BF)
-
-    loads[1].wait()
-    loads[2].wait()
+            total += dot(wide, w[pl.ds(i * 2 * WIDE, 2 * WIDE), 0:512])
+        keys[rows, :] = total[:, 0:256].astype(BF)
+        values[rows, :] = total[:, 256:512].astype(BF)
+
     project(rows_c)
     arrived(x.at[:, rows_p, :], SHARE)
     project(rows_p)
 
     loads[3].wait()
     loads[4].wait()
-    for head in range(2):
-        cols = pl.ds(head * HS, HS)
+    heads = [pl.ds(head * HS, HS) for head in range(2)]
+    for head, cols in enumerate(heads):
         query, grad = qv[:, cols], gv[:, cols]
         key, value = keys[:, cols], values[:, cols]
         tangent = jnp.tanh(dot_nt(query, key) * SCALE / SOFT_CAP)
         weights = jnp.exp(SOFT_CAP * tangent)
         probs = weights / jnp.sum(weights, axis=-1, keepdims=True)
-        probs_low = probs.astype(BF)
-        context[0, :, cols] = dot(probs_low, value).astype(BF)
+        probs_held[head] = probs.astype(BF)
         grad_probs = dot_nt(grad, value)
         inner = jnp.sum(probs * grad_probs, axis=-1, keepdims=True)
-        grad_raw = (probs * (grad_probs - inner) * (1.0 - tangent * tangent) * SCALE).astype(BF)
-        grad_q[0, :, cols] = dot(grad_raw, key).astype(BF)
-        grads[:, cols] = dot_tn(grad_raw, query).astype(BF)
-        grads[:, pl.ds(2 * HS + head * HS, HS)] = dot_tn(probs_low, grad).astype(BF)
-
+        grad_raw = probs * (grad_probs - inner) * (1.0 - tangent * tangent) * SCALE
+        raw_held[head] = grad_raw.astype(BF)
+
+    def key_value_grads(rows):
+        for head, cols in enumerate(heads):
+            grads[rows, cols] = dot_tn(raw_held[head, :, rows], qv[:, cols]).astype(BF)
+            cols_v = pl.ds((2 + head) * HS, HS)
+            grads[rows, cols_v] = dot_tn(probs_held[head, :, rows], gv[:, cols]).astype(BF)
+
+    key_value_grads(rows_p)
     send(grads.at[rows_p], grads_p, OUT_G, G_X, partner)
-
-    pieces = [(i, out) for i in range(4) for out in range(2)]
+    key_value_grads(rows_c)
+
+    pieces = list(range(8))
 
     def weight_grad():
-        i, out = pieces.pop(0)
-        rows = pl.ds(i * 2 * WIDE, 2 * WIDE)
-        wide = jnp.concatenate([x[2 * i], x[2 * i + 1]], axis=1)
-        target = (grad_kw, grad_vw)[out]
-        target[0, rows, :] = dot_tn(wide, grads[:, pl.ds(out * 256, 256)]).astype(BF)
-
-    weight_grad()
-    weight_grad()
+        i = pieces.pop(0)
+        rows = pl.ds(i * WIDE, WIDE)
+        both = dot_tn(x[i], grads[...]).astype(BF)
+        grad_kw[0, rows, :] = both[:, 0:256]
+        grad_vw[0, rows, :] = both[:, 256:512]
+
+    for chip in range(8):
+        own_terms[chip] = dot_nt(grads[rows_c, :], w[pl.ds(chip * WIDE, CA), 0:512])
     arrived(grads_p, G_X)
-    arrived(pair_w, W_X)
-
-    def term(feature, width):
-        span = pl.ds(pl.multiple_of(feature, 128), width)
-        return (
-            dot_nt(grads[rows_c, 0:256], kw[span, :])
-            + dot_nt(grads[rows_c, 256:512], vw[span, :])
-            + dot_nt(grads_p[:, 0:256], pair_w[0, span, :])
-            + dot_nt(grads_p[:, 256:512], pair_w[1, span, :])
-        ).astype(BF)
+    arrived(w.at[:, 512:1024], W_X)
 
     def compute_a(half):
         high = row_of(half * 2)[0]
         for i in range(4):
             chip = high * 4 + i
-            ts[chip, :, 0:CA] = term(chip * WIDE, CA)
+            span = pl.ds(pl.multiple_of(chip * WIDE, 128), CA)
+            ts[chip, :, 0:CA] = (own_terms[chip] + dot_nt(grads_p[...], w[span, 512:1024])).astype(BF)
 
     def scatter(direction, togo, m):
         sign = 1 - 2 * direction
-        index = direction * 16 + (togo - 1) * 4 + m
-        send(a_row(ts, 0, m, z_at(sign * togo)), ring.at[index], OUT_SUM, S_Z + index, z_dev(sign))
-
-    def add(direction, togo, m):
-        sign = 1 - 2 * direction
-        index = direction * 16 + togo * 4 + m
-        held = ring.at[index]
-        arrived(held, S_Z + index)
-        high, low = row_of(m)
-        chips, rows = pl.ds(high * 4, 4), rows16(0, low, z_at(sign * togo))
-        ts[chips, rows, 0:CA] = (ts[chips, rows, 0:CA].astype(F32) + held[...].astype(F32)).astype(BF)
-        if togo:
-            scatter(direction, togo, m)
-
-    def ring_event(*steps):
-        for step in steps:
-            add(0, *RING_A[step])
-            add(1, *RING_B[step])
-
-    def send_b(j):
-        for k in (1, 3, 2):
-            send(
-                b_block(ts, c, 0, along(c, j, k)), recv_q.at[j, k - 1],
-                OUT_TERM, R_Q + j, at(*along(c, 0, k), z, c),
-            )
+        event = (RING_A, RING_B)[direction].index((togo - 1, m))
+        part = a_row(ts, 0, m, z_at(sign * togo))
+        send(part, ring.at[event, direction], OUT_SUM, S_Z + event, z_dev(sign))
+
+    def ring_event(*events):
+        for event in events:
+            arrived(ring.at[event], S_Z + event)
+            for direction, order in enumerate((RING_A, RING_B)):
+                togo, m = order[event]
+                high, low = row_of(m)
+                chips, rows = pl.ds(high * 4, 4), rows16(0, low, z_at((1 - 2 * direction) * togo))
+                total = ts[chips, rows, 0:CA].astype(F32) + ring[event, direction].astype(F32)
+                ts[chips, rows, 0:CA] = total.astype(BF)
+                if togo:
+                    scatter(direction, togo, m)
+
+    def send_b(j, k):
+        send(
+            b_block(ts, c, 0, along(c, j, k)), recv_q.at[j, k - 1],
+            OUT_TERM, R_Q + j, at(*along(c, 0, k), z, c),
+        )
+
+    def compute_b(half):
+        both = jnp.concatenate([grads[rows_c, :], grads_p[...]], axis=1)
+        high = row_of(half * 2)[0]
+        for i in range(4):
+            chip = high * 4 + i
+            span = pl.ds(pl.multiple_of(chip * WIDE + CA, 128), CB)
+            ts[chip, :, CA:WIDE] = dot_nt(both, w[span, :]).astype(BF)
 
     def sum_b(j):
         xx, yy = along(c, j, 0)
@@ -365,10 +357,6 @@
             part = b_block(ts, c, 0, along(c, j, 0))
             send(part, recv_p.at[j - 1], OUT_TERM, R_P, at(*along(c, j, 0), z, c))
 
-    for chip in range(8):
-        ts[chip, :, CA:WIDE] = term(chip * WIDE + CA, CB)
-    for j in (1, 3, 2, 0):
-        send_b(j)
     compute_a(0)
     for m in (0, 1):
         scatter(0, 4, m)
@@ -377,14 +365,49 @@
     for m in (2, 3):
         scatter(0, 3, m)
         scatter(1, 4, m)
-    weight_grad()
-    ring_event(0, 1, 2, 3)
-    sum_b(1)
+    compute_b(1)
+
+    @pl.when(c == 1)
+    def _():
+        for j in (3, 2, 1, 0):
+            for k in (3, 2):
+                send_b(j, k)
+
+    @pl.when(c == 0)
+    def _():
+        for j in (3, 2):
+            for k in (1, 3, 2):
+                send_b(j, k)
+
+    for head, cols in enumerate(heads):
+        context[0, :, cols] = dot(probs_held[head], values[:, cols]).astype(BF)
+        grad_q[0, :, cols] = dot(raw_held[head], keys[:, cols]).astype(BF)
+    weight_grad()
+    ring_event(0, 1)
+    compute_b(0)
+
+    @pl.when(c == 1)
+    def _():
+        for j in (3, 2, 1, 0):
+            send_b(j, 1)
+
+    @pl.when(c == 0)
+    def _():
+        for j in (1, 0):
+            for k in (1, 3, 2):
+                send_b(j, k)
+
+    ring_event(2, 3)
+    weight_grad()
+    weight_grad()
     ring_event(4, 5)
     sum_b(3)
     ring_event(6, 7)
     sum_b(2)
+    weight_grad()
     ring_event(8, 9)
+    sum_b(1)
+    ring_event(10, 11)
     sum_b(0)
 
     def send_plane(m):
@@ -396,12 +419,13 @@
                     OUT_UNIT, S_PL, at(*place, z, c),
                 )
 
-    ring_event(10, 11, 12)
+    ring_event(12)
     send_plane(2)
     send_plane(0)
     ring_event(13)
     send_plane(3)
     send_plane(1)
+    weight_grad()
     rows_b = pl.ds(pl.multiple_of(y_lo * 128, 128), 128)
     total = ts[block, rows_b, CA:WIDE].astype(F32)
     arrived(recv_p, R_P)
@@ -413,7 +437,6 @@
         send(part, recv_z.at[k - 1], OUT_TILE, R_Z, z_dev(k))
     weight_grad()
     weight_grad()
-    weight_grad()
 
     rows_own = rows16(0, y_lo, z)
     total = ts[block, rows_own, 0:CA].astype(F32)
@@ -421,7 +444,6 @@
     for index in range(15):
         total = total + plane[index].astype(F32)
     fin[:, 0:CA] = total.astype(BF)
-    weight_grad()
     total = ts[block, rows_own, CA:WIDE].astype(F32)
     arrived(recv_z, R_Z)
     for index in range(7):
@@ -437,11 +459,11 @@
     grad_x[...] = jnp.where(c == 0, whole[:, 0:PART], whole[:, PART:WIDE]).astype(BF)
 
     left(other_x, OUT_EX)
-    left(kw.at[0 : 30 * UNIT], OUT_UNIT)
+    left(w.at[0 : 30 * UNIT, 0:CA], OUT_UNIT)
     left(x.at[:, 0 : 30 * UNIT, 0:CA], OUT_ROW)
     left(x.at[0, 0 : 14 * UNIT, 0:CB], OUT_TILE)
     left(x.at[:, 0 : 31 * UNIT, 0:CB], OUT_BLOCK)
-    left(pair_w, OUT_W)
+    left(w.at[:, 512:1024], OUT_W)
     left(grads_p, OUT_G)
     left(x.at[0:7, 0:256, 0:CA], OUT_SUM)
     left(x.at[0:4, 0 : 30 * UNIT, 0:CB], OUT_TERM)
@@ -475,11 +497,12 @@
         out_specs=(vmem,) * 5,
         scratch_shapes=[
             pltpu.VMEM((8, SRC, WIDE), BF),
-            pltpu.VMEM((D, 256), BF),
-            pltpu.VMEM((D, 256), BF),
-            pltpu.VMEM((2, D, 256), BF),
+            pltpu.VMEM((D, 1024), BF),
+            pltpu.VMEM((2 * UNIT, PART), BF),
             pltpu.VMEM((UNIT, PART), BF),
-            pltpu.VMEM((UNIT, PART), BF),
+            pltpu.VMEM((2, TGT, SRC), BF),
+            pltpu.VMEM((2, TGT, SRC), BF),
+            pltpu.VMEM((8, HALF, CA), F32),
             pltpu.VMEM((TGT, 256), BF),
             pltpu.VMEM((TGT, 256), BF),
             pltpu.VMEM((SRC, 256), BF),
@@ -490,7 +513,7 @@
             pltpu.VMEM((4, 3, 128, CB), BF),
             pltpu.VMEM((3, 128, CB), BF),
             pltpu.VMEM((7, UNIT, CB), BF),
-            pltpu.VMEM((32, 4, UNIT, CA), BF),
+            pltpu.VMEM((14, 2, 4, UNIT, CA), BF),
             pltpu.VMEM((15, UNIT, CA), BF),
             pltpu.VMEM((UNIT, WIDE), BF),
             pltpu.VMEM((UNIT, WIDE), BF),

time: 69.5 us -> 66.7 us (0.960)
  Pallas kernels: 68.8 us -> 66 us
    pallas_call x1, Pallas kernels: 66.4 us -> 63.5 us  [per_device(): pl.pallas_call(kernel, out_shape=tuple((pltpu.VMEM(shape, BF) for shape i...]
where the time goes in v3:
time: 66.7 us; the launch traced here: 66.6 us
  Pallas kernels  66 us (99%)
    pallas_call x1, Pallas kernels, per_device(): pl.pallas_call(kernel, out_shape=tuple((pltpu.VMEM(shape, BF) for shape i...  63.5 us
    pallas_call x1, Pallas kernels, per_device(): pl.pallas_call(store, out_shape=tuple((jax.ShapeDtypeStruct(shape, BF) fo...  2.45 us

profile of v3, /device:TPU:1, one launch (start us, length us, event | category | flops | bytes accessed | tf_op | source)
XLA Modules:
  0.0 66.6 jit_solution(15462960568774834008)
XLA Ops:
  0.6 63.5 %cross_attention_step.1 = (bf16[1,128,256]{2,1,0:T(8,128)(2,1)S(1)}, bf16[1,128,256]{2,1,0:T(8,128)(2,1)S(1)}, bf16[1,5120,256]{2,1,0:T(8,128)(2,1)S(1)}, bf16[1...) custom-call(bf16[32,320]{1,0:T(8,128)(2,1)} %x_in.1, bf16[1,128,256]{2,1,0:T(8,128)(2,1)} %q_in.1, ...), custom_call_target="tpu_custom_call" | custom-call | flops 8499999744 | bytes 11000000 | tf_op jit(solution)/shard_map/cross_attention_step/pallas_call | solution.py:493
  64.2 2.4 %store_outputs.1 = (bf16[1,128,256]{2,1,0:T(8,128)(2,1)}, bf16[1,128,256]{2,1,0:T(8,128)(2,1)}, bf16[1,5120,256]{2,1,0:T(8,128)(2,1)}, bf16[1,5120,256]{2,1,0:T(8,128)(2,1)}, bf16[32,320]{1,0:T(8,128)(2,1)}) custom-call(bf16[1,128,256]{2,1,0:T(8,128)(2,1)S(1)} %get-tuple-element.10.refs_0_, bf16[1,128,256]{2,1,0:T(8,128)(2,1)S(1)} %get-tuple-element.11.refs_1_, ...), custom_call_target="tpu_custom_call" | custom-call | tf_op jit(solution)/shard_map/store_outputs/pallas_call | solution.py:533

commit v4 on v0

v4 whole, which is shorter than its diff:
```python
import functools

import jax
import jax.numpy as jnp
from jax import lax
from jax.experimental import pallas as pl
from jax.experimental.pallas import tpu as pltpu
from jax.sharding import PartitionSpec as P

MESH = pl.DeviceIdType.MESH
BF = jnp.bfloat16
F32 = jnp.float32

D = 5120
HS = 128
SRC = 512
TGT = 128
WIDE = 640
PART = WIDE // 2
CA = 256
CB = WIDE - CA
UNIT = 32
SOFT_CAP = 20.0
SCALE = HS ** (-0.5)

EX, SHARE, W_X, G_X, FIN = range(5)
A_PL = 5
A_Z = 9
S_Z = 23
S_PL = 37
B_Z = 5
B_P = 6
B_Q = 14
R_Q = 22
R_P = 30
R_Z = 32
RECEIVES = 38

OUT_EX, OUT_W, OUT_G, OUT_FIN, OUT_1, OUT_2, OUT_3 = range(7)
SENDS = 7

GATHER_A = ((0, 0), (0, 1), (0, 3), (0, 2), (1, 0), (1, 1), (1, 3), (1, 2), (2, 0), (2, 1), (2, 3), (2, 2), (3, 0), (3, 1))
GATHER_B = ((0, 0), (0, 3), (0, 2), (0, 1), (1, 3), (1, 2), (1, 0), (1, 1), (2, 3), (2, 2), (2, 0), (2, 1), (3, 3), (3, 2))
RING_A = ((3, 0), (3, 1), (2, 2), (2, 3), (2, 0), (2, 1), (1, 2), (1, 3), (1, 0), (1, 1), (0, 2), (0, 3), (0, 0), (0, 1))
RING_B = ((2, 0), (3, 2), (3, 3), (2, 1), (2, 2), (2, 3), (1, 0), (1, 2), (1, 3), (1, 1), (0, 0), (0, 2), (0, 3), (0, 1))

NT = (((1,), (1,)), ((), ()))
TN = (((0,), (0,)), ((), ()))


def dot(a, b):
    return jnp.dot(a, b, preferred_element_type=F32)


def dot_nt(a, b):
    return lax.dot_general(a, b, NT, preferred_element_type=F32)


def dot_tn(a, b):
    return lax.dot_general(a, b, TN, preferred_element_type=F32)


def kernel(
    x_in, q_in, g_in, kw_in, vw_in,
    context, grad_q, grad_kw, grad_vw, grad_x,
    x, w, own_x, tail, tail_in, probs_held, raw_held, own_a, own_b, qv, gv,
    sums, grads, grads_p, ts_a, ts_b, recv_q, recv_p, recv_z, ring, plane, fin, fin_in,
    send_sem, recv_sem, local_sem,
):
    s = lax.axis_index("section")
    t = lax.axis_index("tensor")
    y_lo, z = lax.div(s, 8), lax.rem(s, 8)
    y_hi, c = lax.div(t, 8), lax.rem(t, 2)
    px = lax.rem(lax.div(t, 2), 4)
    block = y_hi * 4 + px

    def row_of(m):
        return (1 - y_hi if m // 2 else y_hi), (1 - y_lo if m % 2 else y_lo)

    def place(dx, m):
        return (lax.rem(px + dx + 4, 4),) + row_of(m)

    def at(where, zz, cc):
        xx, high, low = where
        return (low * 8 + zz, high * 8 + xx * 2 + cc)

    def along(h, dp, dq):
        return place(dp, abs(dq)) if h == 0 else place(dq, abs(dp))

    here = (px, y_hi, y_lo)
    partner = at(here, z, 1 - c)

    def z_at(k):
        return lax.rem(z + k + 8, 8)

    def rows_of(low, zz):
        first = low * 256 + lax.rem(zz, 2) * 128 + lax.div(zz, 2) * UNIT
        return pl.ds(pl.multiple_of(first, UNIT), UNIT)

    def remote(src, dst, out, slot, device):
        return pltpu.make_async_remote_copy(
            src_ref=src, dst_ref=dst, send_sem=send_sem.at[out], recv_sem=recv_sem.at[slot],
            device_id=device, device_id_type=MESH,
        )

    def send(src, dst, out, slot, device):
        remote(src, dst, out, slot, device).start()

    def arrived(dst, slot):
        remote(dst, dst, OUT_EX, slot, partner).wait_recv()

    def left(src, out):
        remote(src, src, out, EX, partner).wait_send()

    loads = [pltpu.make_async_copy(x_in, own_x, local_sem.at[0])]
    for head in range(2):
        for i, source in enumerate((kw_in, vw_in)):
            for chip in range(8):
                loads.append(
                    pltpu.make_async_copy(
                        source.at[0, chip * WIDE : (chip + 1) * WIDE, head * HS : (head + 1) * HS],
                        w.at[chip, :, (2 * head + i) * HS : (2 * head + i + 1) * HS],
                        local_sem.at[1],
                    )
                )
    loads.append(pltpu.make_async_copy(q_in.at[0], qv, local_sem.at[2]))
    loads.append(pltpu.make_async_copy(g_in.at[0], gv, local_sem.at[3]))
    for load in loads:
        load.start()

    plane_offsets = [(dx, m) for m in (0, 1, 3, 2) for dx in (1, 3, 2, 0) if dx or m]
    barrier = pltpu.get_barrier_semaphore()

    def greet(peers):
        for peer in peers:
            pl.semaphore_signal(barrier, inc=1, device_id=peer, device_id_type=MESH)
        pl.semaphore_wait(barrier, len(peers))

    @pl.when(c == 0)
    def _():
        greet(
            [partner, at(here, z_at(1), 0), at(here, z_at(-1), 0)]
            + [at(place(dx, m), z, 0) for dx, m in plane_offsets]
        )

    @pl.when(c == 1)
    def _():
        greet(
            [partner]
            + [at(here, z_at(k), 1) for k in (1, 7, 2, 6, 3, 5, 4)]
            + [at(place(dx, 0), z, 1) for dx in (1, 3, 2)]
            + [at(place(0, m), z, 1) for m in (1, 3, 2)]
        )

    loads[0].wait()
    own_rows = rows_of(y_lo, z)
    rows_a, rows_b = pl.ds(0, CA), pl.ds(CA, CB)

    def a_unit(ref, where, zz):
        xx, high, low = where
        return ref.at[high * 4 + xx, rows_of(low, zz), 0:CA]

    def a_row(ref, m, zz):
        high, low = row_of(m)
        return ref.at[pl.ds(high * 4, 4), rows_of(low, zz), 0:CA]

    def b_place(h, where):
        xx, high, low = where
        return high * 4 + xx, pl.ds(pl.multiple_of(low * 256 + h * 128, 128), 128)

    def weights_left():
        pltpu.make_async_copy(w.at[:, :, 0:512], w.at[:, :, 0:512], local_sem.at[1]).wait()

    @pl.when(c == 0)
    def _():
        spare = own_x[:, CA:PART].astype(F32)
        tail[...] = jnp.concatenate([spare, jnp.zeros_like(spare)], axis=1).astype(BF)
        send(tail, tail_in, OUT_EX, EX, partner)
        x[block, own_rows, 0:CA] = own_x[:, 0:CA]
        for dx, m in plane_offsets:
            unit = a_unit(x, here, z)
            send(unit, unit, OUT_1, A_PL + m, at(place(dx, m), z, 0))
        weights_left()
        send(w.at[:, rows_b, 0:512], w.at[:, rows_b, 512:1024], OUT_W, W_X, partner)

        def share(m, zz):
            part = a_row(x, m, zz)
            send(part, part, OUT_2, SHARE, partner)

        def pass_on(direction, step, m):
            sign = 1 - 2 * direction
            part = a_row(x, m, z_at(-sign * step))
            event = (GATHER_A, GATHER_B)[direction].index((step, m))
            send(part, part, OUT_2, A_Z + event, at(here, z_at(sign), 0))

        for m in (0, 1, 3, 2):
            high, low = row_of(m)
            units = x.at[pl.ds(high * 4, 4 if m else 3), rows_of(low, z), 0:CA]
            arrived(units, A_PL + m)
            pass_on(0, 0, m)
            pass_on(1, 0, m)
            share(m, z)
        for event in range(14):
            arrived(x.at[:, own_rows, 0:CA], A_Z + event)
            for direction, order in enumerate((GATHER_A, GATHER_B)):
                step, m = order[event]
                if step < 2 or (step == 2 and m // 2 == direction):
                    pass_on(direction, step + 1, m)
                share(m, z_at(-(1 - 2 * direction) * (step + 1)))

    @pl.when(c == 1)
    def _():
        arrived(tail_in, EX)
        spare, own = tail_in[...].astype(F32), own_x[...].astype(F32)
        x[block, own_rows, CA:WIDE] = jnp.concatenate([spare[:, 0 : PART - CA], own], axis=1).astype(BF)
        for k in (4, 3, 5, 2, 6, 1, 7):
            unit = x.at[block, own_rows, rows_b]
            send(unit, unit, OUT_1, B_Z, at(here, z_at(k), 1))
        weights_left()
        send(w.at[:, rows_a, 0:512], w.at[:, rows_a, 512:1024], OUT_W, W_X, partner)

        def part(h, dp, dq):
            chip, rows = b_place(h, along(h, dp, dq))
            return x.at[chip, rows, rows_b]

        def share(h, j, k):
            send(part(h, -j, -k), part(h, -j, -k), OUT_2, SHARE, partner)

        def spread(h, j):
            for k in (1, 3, 2):
                send(part(h, -j, 0), part(h, -j, 0), OUT_2, B_Q + h * 4 + j, at(along(h, 0, k), z, 1))
            share(h, j, 0)

        arrived(x.at[block, 0 : 7 * UNIT, rows_b], B_Z)
        for h in range(2):
            for k in (1, 3, 2):
                send(part(h, 0, 0), part(h, 0, 0), OUT_2, B_P + h * 4 + k, at(along(h, k, 0), z, 1))
        for h in range(2):
            spread(h, 0)
        for j in (1, 3, 2):
            for h in range(2):
                arrived(part(h, -j, 0), B_P + h * 4 + j)
                spread(h, j)
        for j in (0, 1, 3, 2):
            for h in range(2):
                arrived(x.at[0:3, 0:128, rows_b], B_Q + h * 4 + j)
                for k in (1, 3, 2):
                    share(h, j, k)

    def project(first, width, chips):
        wide = jnp.concatenate([x[i, :, first : first + width] for i in chips], axis=1)
        weights = jnp.concatenate([w[i, first : first + width, 0:512] for i in chips], axis=0)
        return dot(wide, weights)

    def project_all(first, width):
        return project(first, width, range(4)) + project(first, width, range(4, 8))

    @pl.when(c == 0)
    def _():
        sums[...] = project_all(0, CA)
        arrived(x.at[:, :, rows_b], SHARE)
        sums[...] += project_all(CA, CB)

    @pl.when(c == 1)
    def _():
        sums[...] = project_all(CA, CB)
        arrived(x.at[:, :, rows_a], SHARE)
        sums[...] += project_all(0, CA)

    loads[-2].wait()
    loads[-1].wait()
    heads = [pl.ds(head * HS, HS) for head in range(2)]

    def projected(head, i):
        first = (2 * head + i) * HS
        return sums[:, first : first + HS].astype(BF)

    for head, cols in enumerate(heads):
        query, grad = qv[:, cols], gv[:, cols]
        key, value = projected(head, 0), projected(head, 1)
        tangent = jnp.tanh(dot_nt(query, key) * SCALE / SOFT_CAP)
        weights = jnp.exp(SOFT_CAP * tangent)
        probs = weights / jnp.sum(weights, axis=-1, keepdims=True)
        probs_low = probs.astype(BF)
        probs_held[head] = probs_low
        grad_probs = dot_nt(grad, value)
        inner = jnp.sum(probs * grad_probs, axis=-1, keepdims=True)
        grad_raw = (probs * (grad_probs - inner) * (1.0 - tangent * tangent) * SCALE).astype(BF)
        raw_held[head] = grad_raw
        pair = pl.ds(head * 256, 256)
        grads[:, head * 256 : head * 256 + HS] = dot_tn(grad_raw, query).astype(BF)
        grads[:, head * 256 + HS : (head + 1) * 256] = dot_tn(probs_low, grad).astype(BF)
        send(grads.at[:, pair], grads_p.at[:, pair], OUT_G, G_X, partner)

    def small_outputs():
        for head, cols in enumerate(heads):
            context[0, :, cols] = dot(probs_held[head], projected(head, 1)).astype(BF)
            grad_q[0, :, cols] = dot(raw_held[head], projected(head, 0)).astype(BF)

    def weight_grad(*chips):
        for i in chips:
            rows = pl.ds(i * WIDE, WIDE)
            both = dot_tn(x[i], grads[...]).astype(BF)
            for head in range(2):
                grad_kw[0, rows, heads[head]] = both[:, head * 256 : head * 256 + HS]
                grad_vw[0, rows, heads[head]] = both[:, head * 256 + HS : (head + 1) * 256]

    @pl.when(c == 0)
    def _():
        for chip in range(8):
            own_a[chip] = dot_nt(grads[...], w[chip, rows_a, 0:512])
        arrived(grads_p, G_X)
        arrived(w.at[:, rows_a, 512:1024], W_X)

        def compute(half):
            high = row_of(half * 2)[0]
            for i in range(4):
                chip = high * 4 + i
                ts_a[chip] = (own_a[chip] + dot_nt(grads_p[...], w[chip, rows_a, 512:1024])).astype(BF)

        def scatter(direction, togo, m):
            sign = 1 - 2 * direction
            event = (RING_A, RING_B)[direction].index((togo - 1, m))
            source = a_row(ts_a, m, z_at(sign * togo))
            send(source, ring.at[event, direction], OUT_3, S_Z + event, at(here, z_at(sign), 0))

        def ring_event(*events):
            for event in events:
                arrived(ring.at[event], S_Z + event)
                for direction, order in enumerate((RING_A, RING_B)):
                    togo, m = order[event]
                    high, low = row_of(m)
                    chips, rows = pl.ds(high * 4, 4), rows_of(low, z_at((1 - 2 * direction) * togo))
                    total = ts_a[chips, rows, :].astype(F32) + ring[event, direction].astype(F32)
                    ts_a[chips, rows, :] = total.astype(BF)
                    if togo:
                        scatter(direction, togo, m)

        def send_plane(m):
            for dx in (2, 1, 3, 0):
                if dx or m:
                    where = place(dx, m)
                    send(a_unit(ts_a, where, z), plane.at[m * 4 + dx - 1], OUT_1, S_PL, at(where, z, 0))

        compute(0)
        for m in (0, 1):
            scatter(0, 4, m)
            scatter(1, 3, m)
        compute(1)
        for m in (2, 3):
            scatter(0, 3, m)
            scatter(1, 4, m)
        small_outputs()
        weight_grad(0)
        ring_event(0, 1)
        weight_grad(1)
        ring_event(2, 3)
        weight_grad(2)
        ring_event(4, 5)
        weight_grad(3)
        ring_event(6, 7)
        weight_grad(4)
        ring_event(8, 9)
        ring_event(10, 11, 12)
        send_plane(2)
        send_plane(0)
        ring_event(13)
        send_plane(3)
        send_plane(1)
        weight_grad(5, 6, 7)
        total = ts_a[block, own_rows, :].astype(F32)
        arrived(plane, S_PL)
        for index in range(15):
            total = total + plane[index].astype(F32)
        grad_x[:, 0:CA] = total.astype(BF)
        arrived(fin_in, FIN)
        grad_x[:, CA:PART] = fin_in[:, 0 : PART - CA]
        left(tail, OUT_EX)
        left(x.at[0:2, 0:480, 0:CA], OUT_1)
        left(w.at[:, rows_b, 0:512], OUT_W)
        left(x.at[:, 0:480, 0:512], OUT_2)
        left(x.at[0:7, :, 0:CA], OUT_3)

    @pl.when(c == 1)
    def _():
        def span(half):
            high = row_of(half * 2)[0]
            return [high * 4 + i for i in range(4)]

        for i, chip in enumerate(span(1)):
            own_b[i] = dot_nt(grads[...], w[chip, rows_b, 0:512])
        arrived(grads_p, G_X)
        arrived(w.at[:, rows_b, 512:1024], W_X)

        def send_q(h, j, k):
            chip, rows = b_place(h, along(h, j, k))
            send(
                ts_b.at[chip, rows], recv_q.at[h, j, k - 1],
                OUT_3, R_Q + h * 4 + j, at(along(h, 0, k), z, 1),
            )

        def sum_q(j):
            for h in range(2):
                chip, rows = b_place(h, along(h, j, 0))
                total = ts_b[chip, rows, :].astype(F32)
                arrived(recv_q.at[h, j], R_Q + h * 4 + j)
                for k in range(3):
                    total = total + recv_q[h, j, k].astype(F32)
                ts_b[chip, rows, :] = total.astype(BF)
                if j:
                    send(
                        ts_b.at[chip, rows], recv_p.at[h, j - 1],
                        OUT_3, R_P + h, at(along(h, j, 0), z, 1),
                    )

        for i, chip in enumerate(span(1)):
            ts_b[chip] = (own_b[i] + dot_nt(grads_p[...], w[chip, rows_b, 512:1024])).astype(BF)
        for j in (3, 2, 1, 0):
            for k in (3, 2):
                send_q(0, j, k)
            if j > 1:
                for k in (1, 3, 2):
                    send_q(1, j, k)
        both = jnp.concatenate([grads[...], grads_p[...]], axis=1)
        for chip in span(0):
            ts_b[chip] = dot_nt(both, w[chip, rows_b, :]).astype(BF)
        for j in (3, 2, 1, 0):
            send_q(0, j, 1)
            if j < 2:
                for k in (1, 3, 2):
                    send_q(1, j, k)
        small_outputs()
        weight_grad(0, 1, 2)
        sum_q(3)
        weight_grad(3)
        sum_q(2)
        weight_grad(4)
        sum_q(1)
        weight_grad(5)
        sum_q(0)
        for h in range(2):
            chip, rows = b_place(h, here)
            total = ts_b[chip, rows, :].astype(F32)
            arrived(recv_p.at[h], R_P + h)
            for j in range(3):
                total = total + recv_p[h, j].astype(F32)
            ts_b[chip, rows, :] = total.astype(BF)
        for k in (4, 3, 5, 2, 6, 1, 7):
            source = ts_b.at[block, rows_of(y_lo, z_at(k))]
            send(source, recv_z.at[k - 1], OUT_1, R_Z, at(here, z_at(k), 1))
        weight_grad(6, 7)
        total = ts_b[block, own_rows, :].astype(F32)
        arrived(recv_z, R_Z)
        for index in range(7):
            total = total + recv_z[index].astype(F32)
        fin[...] = total[:, 0:HS].astype(BF)
        send(fin, fin_in, OUT_FIN, FIN, partner)
        grad_x[...] = total[:, PART - CA : CB].astype(BF)
        left(x.at[0, 0 : 14 * UNIT, 0:CB], OUT_1)
        left(w.at[:, rows_a, 0:512], OUT_W)
        left(w.at[:, 0:496, 0:768], OUT_2)
        left(x.at[:, 0:480, 0:CB], OUT_3)
        left(fin, OUT_FIN)

    left(grads, OUT_G)


def store(*refs):
    sources, targets, sems = refs[:5], refs[5:10], refs[10]
    copies = [
        pltpu.make_async_copy(source, target, sems.at[i])
        for i, (source, target) in enumerate(zip(sources, targets))
    ]
    for copy in copies:
        copy.start()
    for copy in copies:
        copy.wait()


def per_device(encoder_states, queries, grad_context, key_weight, value_weight):
    anywhere = pl.BlockSpec(memory_space=pl.ANY)
    vmem = pl.BlockSpec(memory_space=pltpu.VMEM)
    shapes = ((1, TGT, 256), (1, TGT, 256), (1, D, 256), (1, D, 256), (32, PART))
    inputs = [
        pltpu.with_memory_space_constraint(array, pltpu.HBM)
        for array in (encoder_states, queries, grad_context, key_weight, value_weight)
    ]
    results = pl.pallas_call(
        kernel,
        out_shape=tuple(pltpu.VMEM(shape, BF) for shape in shapes),
        in_specs=[pl.BlockSpec(memory_space=pltpu.HBM)] * 5,
        out_specs=(vmem,) * 5,
        scratch_shapes=[
            pltpu.VMEM((8, SRC, WIDE), BF),
            pltpu.VMEM((8, WIDE, 1024), BF),
            pltpu.VMEM((UNIT, PART), BF),
            pltpu.VMEM((UNIT, HS), BF),
            pltpu.VMEM((UNIT, HS), BF),
            pltpu.VMEM((2, TGT, SRC), BF),
            pltpu.VMEM((2, TGT, SRC), BF),
            pltpu.VMEM((8, SRC, CA), F32),
            pltpu.VMEM((4, SRC, CB), F32),
            pltpu.VMEM((TGT, 256), BF),
            pltpu.VMEM((TGT, 256), BF),
            pltpu.VMEM((SRC, 512), F32),
            pltpu.VMEM((SRC, 512), BF),
            pltpu.VMEM((SRC, 512), BF),
            pltpu.VMEM((8, SRC, CA), BF),
            pltpu.VMEM((8, SRC, CB), BF),
            pltpu.VMEM((2, 4, 3, 128, CB), BF),
            pltpu.VMEM((2, 3, 128, CB), BF),
            pltpu.VMEM((7, UNIT, CB), BF),
            pltpu.VMEM((14, 2, 4, UNIT, CA), BF),
            pltpu.VMEM((15, UNIT, CA), BF),
            pltpu.VMEM((UNIT, HS), BF),
            pltpu.VMEM((UNIT, HS), BF),
            pltpu.SemaphoreType.DMA((SENDS,)),
            pltpu.SemaphoreType.DMA((RECEIVES,)),
            pltpu.SemaphoreType.DMA((4,)),
        ],
        compiler_params=pltpu.CompilerParams(
            collective_id=0, has_side_effects=True, vmem_limit_bytes=48 << 20
        ),
        cost_estimate=pl.CostEstimate(
            flops=8_500_000_000, bytes_accessed=11_000_000, transcendentals=262_144
        ),
        name="cross_attention_step",
    )(*inputs)
    results = [pltpu.with_memory_space_constraint(result, pltpu.VMEM) for result in results]
    return pl.pallas_call(
        store,
        out_shape=tuple(jax.ShapeDtypeStruct(shape, BF) for shape in shapes),
        in_specs=[vmem] * 5,
        out_specs=(anywhere,) * 5,
        scratch_shapes=[pltpu.SemaphoreType.DMA((5,))],
        compiler_params=pltpu.CompilerParams(vmem_limit_bytes=4 << 20),
        name="store_outputs",
    )(*results)


def solution(mesh):
    in_specs = (
        P("section", "tensor"),
        P("section", None, "tensor"),
        P("section", None, "tensor"),
        P("section", None, "tensor"),
        P("section", None, "tensor"),
    )
    out_specs = (
        P("section", None, "tensor"),
        P("section", None, "tensor"),
        P("section", None, "tensor"),
        P("section", None, "tensor"),
        P("section", "tensor"),
    )
    return jax.shard_map(
        per_device, mesh=mesh, in_specs=in_specs, out_specs=out_specs, check_vma=False
    )
```

time: 295 us -> 63.7 us (0.22)
  the two profiles are of different devices: /device:TPU:1 before, /device:TPU:2 now
where the time goes in v4:
time: 63.7 us; the launch traced here: 63.6 us
  Pallas kernels  62.8 us (99%)
  between operations  0.8 us (1%)
    pallas_call x1, Pallas kernels, per_device(): pl.pallas_call(kernel, out_shape=tuple((pltpu.VMEM(shape, BF) for shape i...  60.4 us
    pallas_call x1, Pallas kernels, per_device(): pl.pallas_call(store, out_shape=tuple((jax.ShapeDtypeStruct(shape, BF) fo...  2.45 us

profile of v4, /device:TPU:2, one launch (start us, length us, event | category | flops | bytes accessed | tf_op | source)
XLA Modules:
  0.0 63.6 jit_solution(912351923924232321)
XLA Ops:
  0.6 60.4 %cross_attention_step.1 = (bf16[1,128,256]{2,1,0:T(8,128)(2,1)S(1)}, bf16[1,128,256]{2,1,0:T(8,128)(2,1)S(1)}, bf16[1,5120,256]{2,1,0:T(8,128)(2,1)S(1)}, bf16[1...) custom-call(bf16[32,320]{1,0:T(8,128)(2,1)} %x_in.1, bf16[1,128,256]{2,1,0:T(8,128)(2,1)} %q_in.1, ...), custom_call_target="tpu_custom_call" | custom-call | flops 8499999744 | bytes 11000000 | tf_op jit(solution)/shard_map/cross_attention_step/pallas_call | solution.py:488
  61.0 2.4 %store_outputs.1 = (bf16[1,128,256]{2,1,0:T(8,128)(2,1)}, bf16[1,128,256]{2,1,0:T(8,128)(2,1)}, bf16[1,5120,256]{2,1,0:T(8,128)(2,1)}, bf16[1,5120,256]{2,1,0:T(8,128)(2,1)}, bf16[32,320]{1,0:T(8,128)(2,1)}) custom-call(bf16[1,128,256]{2,1,0:T(8,128)(2,1)S(1)} %get-tuple-element.10.refs_0_, bf16[1,128,256]{2,1,0:T(8,128)(2,1)S(1)} %get-tuple-element.11.refs_1_, ...), custom_call_target="tpu_custom_call" | custom-call | tf_op jit(solution)/shard_map/store_outputs/pallas_call | solution.py:530

commit v5 on v4

--- a/solution.py
+++ b/solution.py
@@ -40,9 +40,9 @@
 SENDS = 7
 
 GATHER_A = ((0, 0), (0, 1), (0, 3), (0, 2), (1, 0), (1, 1), (1, 3), (1, 2), (2, 0), (2, 1), (2, 3), (2, 2), (3, 0), (3, 1))
-GATHER_B = ((0, 0), (0, 3), (0, 2), (0, 1), (1, 3), (1, 2), (1, 0), (1, 1), (2, 3), (2, 2), (2, 0), (2, 1), (3, 3), (3, 2))
+GATHER_B = ((0, 0), (0, 1), (0, 3), (0, 2), (1, 0), (1, 1), (1, 3), (1, 2), (2, 0), (2, 1), (2, 3), (2, 2), (3, 3), (3, 2))
 RING_A = ((3, 0), (3, 1), (2, 2), (2, 3), (2, 0), (2, 1), (1, 2), (1, 3), (1, 0), (1, 1), (0, 2), (0, 3), (0, 0), (0, 1))
-RING_B = ((2, 0), (3, 2), (3, 3), (2, 1), (2, 2), (2, 3), (1, 0), (1, 2), (1, 3), (1, 1), (0, 0), (0, 2), (0, 3), (0, 1))
+RING_B = ((2, 0), (2, 1), (3, 2), (3, 3), (1, 0), (1, 1), (2, 2), (2, 3), (0, 0), (0, 1), (1, 2), (1, 3), (0, 2), (0, 3))
 
 NT = (((1,), (1,)), ((), ()))
 TN = (((0,), (0,)), ((), ()))
@@ -171,6 +171,19 @@
     def weights_left():
         pltpu.make_async_copy(w.at[:, :, 0:512], w.at[:, :, 0:512], local_sem.at[1]).wait()
 
+    def project(first, width, chips, rows):
+        wide = jnp.concatenate([x[i, rows, first : first + width] for i in chips], axis=1)
+        weights = jnp.concatenate([w[i, first : first + width, 0:512] for i in chips], axis=0)
+        return dot(wide, weights)
+
+    def project_all(first, width, rows=slice(None)):
+        return project(first, width, range(4), rows) + project(first, width, range(4, 8), rows)
+
+    def project_parity(odd):
+        for low in range(2):
+            rows = pl.ds(pl.multiple_of(low * 256 + odd * 128, 128), 128)
+            sums[rows, :] = project_all(0, CA, rows)
+
     @pl.when(c == 0)
     def _():
         spare = own_x[:, CA:PART].astype(F32)
@@ -200,13 +213,19 @@
             pass_on(0, 0, m)
             pass_on(1, 0, m)
             share(m, z)
-        for event in range(14):
-            arrived(x.at[:, own_rows, 0:CA], A_Z + event)
-            for direction, order in enumerate((GATHER_A, GATHER_B)):
-                step, m = order[event]
-                if step < 2 or (step == 2 and m // 2 == direction):
-                    pass_on(direction, step + 1, m)
-                share(m, z_at(-(1 - 2 * direction) * (step + 1)))
+        def ring_arrived(*events):
+            for event in events:
+                arrived(x.at[:, own_rows, 0:CA], A_Z + event)
+                pair = [order[event] for order in (GATHER_A, GATHER_B)]
+                for direction, (step, m) in enumerate(pair):
+                    if step < 2 or (step == 2 and m // 2 == direction):
+                        pass_on(direction, step + 1, m)
+                for direction, (step, m) in enumerate(pair):
+                    share(m, z_at(-(1 - 2 * direction) * (step + 1)))
+
+        ring_arrived(*range(12))
+        project_parity(1 - lax.rem(z, 2))
+        ring_arrived(12, 13)
 
     @pl.when(c == 1)
     def _():
@@ -247,17 +266,9 @@
                 for k in (1, 3, 2):
                     share(h, j, k)
 
-    def project(first, width, chips):
-        wide = jnp.concatenate([x[i, :, first : first + width] for i in chips], axis=1)
-        weights = jnp.concatenate([w[i, first : first + width, 0:512] for i in chips], axis=0)
-        return dot(wide, weights)
-
-    def project_all(first, width):
-        return project(first, width, range(4)) + project(first, width, range(4, 8))
-
     @pl.when(c == 0)
     def _():
-        sums[...] = project_all(0, CA)
+        project_parity(lax.rem(z, 2))
         arrived(x.at[:, :, rows_b], SHARE)
         sums[...] += project_all(CA, CB)
 
@@ -350,24 +361,21 @@
         for m in (2, 3):
             scatter(0, 3, m)
             scatter(1, 4, m)
-        small_outputs()
-        weight_grad(0)
-        ring_event(0, 1)
-        weight_grad(1)
+        ring_event(0)
+        ring_event(1)
         ring_event(2, 3)
-        weight_grad(2)
         ring_event(4, 5)
-        weight_grad(3)
         ring_event(6, 7)
-        weight_grad(4)
         ring_event(8, 9)
-        ring_event(10, 11, 12)
+        ring_event(10, 11)
+        ring_event(12)
         send_plane(2)
         send_plane(0)
         ring_event(13)
         send_plane(3)
         send_plane(1)
-        weight_grad(5, 6, 7)
+        small_outputs()
+        weight_grad(*range(8))
         total = ts_a[block, own_rows, :].astype(F32)
         arrived(plane, S_PL)
         for index in range(15):

time: 63.7 us -> 63.2 us (level)
  the two profiles are of different devices: /device:TPU:2 before, /device:TPU:32 now
where the time goes in v5:
time: 63.2 us; the launch traced here: 63.1 us
  Pallas kernels  62.3 us (99%)
  between operations  0.8 us (1%)
    pallas_call x1, Pallas kernels, per_device(): pl.pallas_call(kernel, out_shape=tuple((pltpu.VMEM(shape, BF) for shape i...  59.9 us
    pallas_call x1, Pallas kernels, per_device(): pl.pallas_call(store, out_shape=tuple((jax.ShapeDtypeStruct(shape, BF) fo...  2.45 us

profile of v5, /device:TPU:32, one launch (start us, length us, event | category | flops | bytes accessed | tf_op | source)
XLA Modules:
  0.0 63.1 jit_solution(15563143539304059656)
XLA Ops:
  0.6 59.9 %cross_attention_step.1 = (bf16[1,128,256]{2,1,0:T(8,128)(2,1)S(1)}, bf16[1,128,256]{2,1,0:T(8,128)(2,1)S(1)}, bf16[1,5120,256]{2,1,0:T(8,128)(2,1)S(1)}, bf16[1...) custom-call(bf16[32,320]{1,0:T(8,128)(2,1)} %x_in.1, bf16[1,128,256]{2,1,0:T(8,128)(2,1)} %q_in.1, ...), custom_call_target="tpu_custom_call" | custom-call | flops 8499999744 | bytes 11000000 | tf_op jit(solution)/shard_map/cross_attention_step/pallas_call | solution.py:496
  60.5 2.4 %store_outputs.1 = (bf16[1,128,256]{2,1,0:T(8,128)(2,1)}, bf16[1,128,256]{2,1,0:T(8,128)(2,1)}, bf16[1,5120,256]{2,1,0:T(8,128)(2,1)}, bf16[1,5120,256]{2,1,0:T(8,128)(2,1)}, bf16[32,320]{1,0:T(8,128)(2,1)}) custom-call(bf16[1,128,256]{2,1,0:T(8,128)(2,1)S(1)} %get-tuple-element.10.refs_0_, bf16[1,128,256]{2,1,0:T(8,128)(2,1)S(1)} %get-tuple-element.11.refs_1_, ...), custom_call_target="tpu_custom_call" | custom-call | tf_op jit(solution)/shard_map/store_outputs/pallas_call | solution.py:538
